TPU v7x, 512 devices: a whole 4x8x8 slice. The times are simulated.
512 devices in a mesh: cell: 16 (over x_hi, z), sta: 32 (over x_lo, y, core).
Axes of the slice: x: 4 (x_hi: 2, x_lo: 2; x = x_hi * 2 + x_lo), y: 8, z: 8, core: 2. Of those that a mesh axis runs over, the one named last changes fastest.
Arguments:
- cell_index: int32 [3, 2048], P(None, 'cell'), may hold values from 0 to 127
- station_xyz: float32 [3, 256], P(None, 'sta'), may hold values from 0 to 2
- w_cell: float32 [3, 512], replicated, may hold values from -2.5 to 2.5
- w_station: float32 [3, 512], replicated, may hold values from -2.5 to 2.5
- bias_in: float32 [512], replicated, may hold values from -4 to 4
- w_hidden: bfloat16 [2, 512, 512], replicated, may hold values from -0.25 to 0.25
- bias_hidden: float32 [2, 512], replicated, may hold values from -3 to 3
- w_out: bfloat16 [512], replicated, may hold values from -0.25 to 0.25
- pick_mask: int32 [2048, 256], P('cell', 'sta'), may hold values 0 or 1
- arrival: float32 [2048, 256], P('cell', 'sta'), may hold values from 0 to 4
- quality: float32 [2048, 256], P('cell', 'sta'), may hold values from 0.002 to 2
Outputs:
- log_posterior: float32 [2048, 2048], P('sta', 'cell')
All inputs are finite; a program needn't handle non-finite values. No bound on the sum of `pick_mask` on one device may be relied on, other than what follows from the above.
Results may differ from a plain program's by a relative error of at most 0.0011.
The roundings to bfloat16 on the way count: a program that leaves them out, or rounds other values in their place, can miss the bound.
Values sent between devices are 32-bit elements; how exact they have to be, the bound alone decides.
No kernel may reach another device: no remote copies, remote signals or barrier semaphores. Data moves between devices by JAX's collectives and lax.ppermute only.
A program may use at most 64 MiB of HBM per device.

v0:
```python
import jax
import jax.numpy as jnp
from jax import lax
from jax.sharding import PartitionSpec as P

grid_step = 0.015625


def travel_times(cell_index, station_xyz, w_cell, w_station, bias_in, w_hidden, bias_hidden, w_out):
    highest = lax.Precision.HIGHEST
    cell_xyz = cell_index.astype(jnp.float32) * grid_step
    cell_count = cell_xyz.shape[1]
    station_count = station_xyz.shape[1]
    hidden_width = w_cell.shape[1]
    cell_rows = jnp.einsum("kc,kh->ch", cell_xyz, w_cell, precision=highest) + bias_in
    station_rows = jnp.einsum("ks,kh->sh", station_xyz, w_station, precision=highest)
    block_size = max(1, min(cell_count, 16384 // station_count))
    block_count = cell_count // block_size

    def one_block(block_item):
        rows_here, positions = block_item
        hidden = jax.nn.elu(rows_here[:, None, :] + station_rows[None, :, :]).astype(jnp.bfloat16)
        hidden = hidden.reshape(block_size * station_count, hidden_width)
        for layer_id in range(w_hidden.shape[0]):
            hidden = jax.nn.elu(
                jnp.dot(hidden, w_hidden[layer_id], preferred_element_type=jnp.float32)
                + bias_hidden[layer_id]
            ).astype(jnp.bfloat16)
        output_raw = jnp.dot(hidden, w_out, preferred_element_type=jnp.float32).reshape(
            block_size, station_count
        )
        offsets = positions[:, :, None] - station_xyz[None, :, :]
        distance = jnp.sqrt(jnp.sum(offsets * offsets, axis=1))
        return distance * (0.25 + jax.nn.softplus(output_raw))

    blocks = (
        cell_rows.reshape(block_count, block_size, hidden_width),
        cell_xyz.T.reshape(block_count, block_size, 3),
    )
    result = lax.map(one_block, blocks)
    return result.reshape(cell_count, station_count)


def misfit_terms(arrivals, weights, travel):
    highest = lax.Precision.HIGHEST
    weighted = weights * arrivals
    curv = jnp.einsum("es,cs->ec", weights, travel * travel, precision=highest) - 2.0 * jnp.einsum(
        "es,cs->ec", weighted, travel, precision=highest
    )
    lin = jnp.einsum("es,cs->ec", weights, travel, precision=highest)
    return (
        curv,
        lin,
        jnp.sum(weighted * arrivals, axis=1),
        jnp.sum(weighted, axis=1),
        jnp.sum(weights, axis=1),
    )


def per_device(
    cell_index,
    station_xyz,
    w_cell,
    w_station,
    bias_in,
    w_hidden,
    bias_hidden,
    w_out,
    pick_mask,
    arrival,
    quality,
):
    weight = pick_mask.astype(jnp.float32) * quality
    all_arrivals, all_weights = (
        lax.all_gather(arrival, "cell", axis=0, tiled=True),
        lax.all_gather(weight, "cell", axis=0, tiled=True),
    )
    travel = travel_times(
        cell_index, station_xyz, w_cell, w_station, bias_in, w_hidden, bias_hidden, w_out
    )
    terms = misfit_terms(all_arrivals, all_weights, travel)
    summed = lax.psum((terms[0], terms[1], terms[2], terms[3], terms[4]), "sta")
    row_count = summed[0].shape[0] // lax.axis_size("sta")
    row_start = lax.axis_index("sta") * row_count
    curv, lin, sq_sum, mean_sum, total_w = [
        lax.dynamic_slice_in_dim(member, row_start, row_count, 0) for member in summed
    ]
    centered = mean_sum[:, None] - lin
    misfit = sq_sum[:, None] + curv - centered * centered / total_w[:, None]
    logit = -0.5 * misfit
    peak = lax.pmax(jnp.max(logit, axis=1), "cell")
    total = lax.psum(jnp.sum(jnp.exp(logit - peak[:, None]), axis=1), "cell")
    return logit - peak[:, None] - jnp.log(total)[:, None]


def solution(mesh):
    in_specs = (
        P(None, "cell"),
        P(None, "sta"),
        P(),
        P(),
        P(),
        P(),
        P(),
        P(),
        P("cell", "sta"),
        P("cell", "sta"),
        P("cell", "sta"),
    )
    out_specs = P("sta", "cell")
    return jax.shard_map(
        per_device, mesh=mesh, in_specs=in_specs, out_specs=out_specs, check_vma=False
    )
```

profile of v0, /device:TPU:6, one launch (start us, length us, event | category | flops | bytes accessed | tf_op | source)
XLA Modules:
  0.0 422.8 jit_solution(5019671365317209401)
XLA Ops:
  6.5 0.0 copy-start
  6.5 0.0 all-reduce.4.cloned.1.call-start
  6.5 0.7 reshape.39
  7.2 0.7 fusion.26
  7.9 0.8 fusion.36
  8.7 0.8 multiply_reduce_fusion.2
  9.4 0.9 fusion.37
  10.4 0.7 convert_multiply_fusion
  11.1 45.7 %all_gather.6 = f32[2048,8]{0,1:T(8,128)S(1)} all-gather(f32[128,8]{0,1:T(8,128)S(1)} %convert_multiply_fusion), channel_id=1, replica_groups=mesh['cell'=16,'sta'=32] {'cell'}, dimensions={0}, use_global_device_ids=true | all-gather | bytes 69632 | tf_op jit(solution)/shard_map/all_gather | solution.py:76
  56.8 0.0 copy-done
  56.8 1.1 convolution_add_fusion
  57.9 0.0 copy-start.2
  58.0 2.9 fusion.4
  60.8 0.0 copy-done.2
  60.9 1.5 fusion.7
  62.4 0.1 reshape.38
  62.5 2.8 fusion.31
  65.4 1.8 fusion.24
  67.2 35.9 %all_gather.7 = f32[2048,8]{0,1:T(8,128)S(1)} all-gather(f32[128,8]{0,1:T(8,128)S(1)} %copy-done.1), channel_id=1, replica_groups=mesh['cell'=16,'sta'=32] {'cell'}, dimensions={0}, use_global_device_ids=true | all-gather | bytes 69632 | tf_op jit(solution)/shard_map/all_gather | solution.py:75
  103.0 2.8 fusion
  105.8 0.0 all-reduce.4.cloned.1.call-update
  105.9 0.1 multiply_reduce_fusion
  105.9 104.6 %all-reduce = (f32[2048]{0:T(1024)S(1)}, f32[2048]{0:T(1024)S(1)}, f32[2048]{0:T(1024)S(1)}) all-reduce(f32[2048]{0:T(1024)S(1)} %get-tuple-element.23, f32[2048]{0:T(1024)S(1)} %get-tuple-element.22, f32[2048]{0:T(1024)S(1)} %get-tuple-element.21), channel_id=1, replica_groups=mesh['cell'=16,'sta'=32] {'sta'}, use_global_device_ids=true, to_apply=%region_8.9 | all-reduce | flops 6144 | bytes 49152 | tf_op jit(solution)/shard_map/psum | solution.py:82
  210.5 0.1 dynamic_slice.25
  210.6 0.1 dynamic_slice.23
  210.7 0.1 dynamic_slice.21
  210.7 125.2 %all-reduce.4.cloned.1.call-done = (f32[2048,128]{1,0:T(8,128)}, f32[2048,128]{1,0:T(8,128)}) async-done(((f32[2048,128]{1,0:T(8,128)}, f32[2048,128]{1,0:T(8,128)}), (f32[2048,128]{1,0:T(8,128)}, f32[2048,128]{1,0:T(8,128)})) %all-reduce.4.cloned.1.call-update) | async-done | bytes 2097168 | tf_op jit(solution)/shard_map/psum | solution.py:82
  336.0 1.0 fusion.35
  336.9 41.5 %pmax.7 = f32[64]{0:T(128)S(1)} all-reduce(f32[64]{0:T(128)S(1)} %get-tuple-element.40), channel_id=1, replica_groups=mesh['cell'=16,'sta'=32] {'cell'}, use_global_device_ids=true, to_apply=%region_10.11 | all-reduce | flops 64 | bytes 512 | tf_op jit(solution)/shard_map/pmax | solution.py:91
  378.4 0.2 exponential_reduce_fusion
  378.6 36.6 %psum.47 = f32[64]{0:T(128)S(1)} all-reduce(f32[64]{0:T(128)S(1)} %exponential_reduce_fusion), channel_id=1, replica_groups=mesh['cell'=16,'sta'=32] {'cell'}, use_global_device_ids=true, to_apply=%region_12.13 | all-reduce | flops 64 | bytes 512 | tf_op jit(solution)/shard_map/psum | solution.py:92
  415.3 0.7 subtract_subtract_fusion
  (4 shorter events, 0.1 us)
Async XLA Ops:
  6.5 50.3 %copy-start = (f32[3,512]{1,0:T(4,128)S(1)}, f32[3,512]{1,0:T(4,128)}, u32[]{:S(2)}) copy-start(f32[3,512]{1,0:T(4,128)} %param.13) | copy-start | bytes 18436
  6.5 329.4 %all-reduce.4.cloned.1.call-start = ((), (), s32[]{:S(2)}) async-start(), calls=%async_computation | async-start | bytes 4194304 | tf_op jit(solution)/shard_map/psum | solution.py:82
  57.9 2.9 copy-start.2
  62.5 4.6 %copy-start.1 = (f32[128,8]{0,1:T(8,128)S(1)}, f32[128,8]{0,1:T(8,128)}, u32[]{:S(2)}) copy-start(f32[128,8]{0,1:T(8,128)} %param.20) | copy-start | bytes 12292
Sparse Core Ops, SparseCore 0:
  106.0 229.9 all-reduce.3
where the time goes:
time: 424 us; the launch traced here: 423 us
  blocking collectives  264 us (62%)
  waiting for transfers between devices  125 us (29%)
  matrix products  13.9 us (3%)
  between operations  13.5 us (3%)
    psum x1, waiting for transfers between devices, per_device(): summed = lax.psum((terms[0], terms[1], terms[2], terms[3], terms[4]), 'sta')  125 us
    psum x1, blocking collectives, per_device(): summed = lax.psum((terms[0], terms[1], terms[2], terms[3], terms[4]), 'sta')  105 us
    all_gather x1, blocking collectives, per_device(): lax.all_gather(weight, 'cell', axis=0, tiled=True)  45.7 us
    pmax x1, blocking collectives, per_device(): peak = lax.pmax(jnp.max(logit, axis=1), 'cell')  41.5 us
    psum x1, blocking collectives, per_device(): total = lax.psum(jnp.sum(jnp.exp(logit - peak[:, None]), axis=1), 'cell')  36.6 us
    all_gather x1, blocking collectives, per_device(): lax.all_gather(arrival, 'cell', axis=0, tiled=True)  35.9 us
  transfers between devices with their start and end apart: 1, of which 1 were waited for; matrix products, arithmetic and copies ran while one was open for 0% of the time, Pallas kernels for 0%

commit v1 on v0

v1 whole, which is shorter than its diff:
```python
import jax
import jax.numpy as jnp
from jax import lax
from jax.experimental import pallas as pl
from jax.experimental.pallas import tpu as pltpu
from jax.sharding import PartitionSpec as P

grid_step = 0.015625
highest = lax.Precision.HIGHEST


def elu(x):
    return jnp.where(x > 0.0, x, jnp.exp(jnp.minimum(x, 0.0)) - 1.0)


def pack_kernel(mask_ref, arrival_ref, quality_ref, out_ref):
    weight = mask_ref[...].astype(jnp.float32) * quality_ref[...]
    arrival = arrival_ref[...]
    half = weight.shape[1] // 2
    for h in range(2):
        part = slice(h * half, (h + 1) * half)
        block = jnp.concatenate([weight[:, part], arrival[:, part]], axis=1)
        for peer in range(out_ref.shape[0]):
            out_ref[peer, h] = block


def travel_kernel(
    cell_ref,
    station_ref,
    w_cell_ref,
    w_station_ref,
    bias_in_ref,
    w_hidden_ref,
    bias_hidden_ref,
    w_out_ref,
    out_ref,
    hidden_ref,
):
    stations = station_ref.shape[1]
    cells = cell_ref.shape[1]
    cell = cell_ref[...].astype(jnp.float32) * grid_step
    cell_columns = cell.T
    station_columns = station_ref[...].T
    cell_rows = jnp.broadcast_to(bias_in_ref[...], (cells, bias_in_ref.shape[1]))
    station_rows = jnp.zeros((stations, bias_in_ref.shape[1]), jnp.float32)
    distance = jnp.zeros((stations, cells), jnp.float32)
    for k in range(3):
        cell_rows = cell_rows + cell_columns[:, k : k + 1] * w_cell_ref[k : k + 1, :]
        station_rows = station_rows + station_columns[:, k : k + 1] * w_station_ref[k : k + 1, :]
        offset = cell[k : k + 1, :] - station_columns[:, k : k + 1]
        distance = distance + offset * offset
    distance = jnp.sqrt(distance)
    for s in range(stations):
        hidden_ref[s * cells : (s + 1) * cells, :] = elu(cell_rows + station_rows[s : s + 1, :]).astype(
            jnp.bfloat16
        )
    hidden = hidden_ref[...]
    for layer in range(w_hidden_ref.shape[0]):
        hidden = elu(
            jnp.dot(hidden, w_hidden_ref[layer], preferred_element_type=jnp.float32)
            + bias_hidden_ref[layer : layer + 1, :]
        ).astype(jnp.bfloat16)
    raw = lax.dot_general(
        w_out_ref[...], hidden, (((1,), (1,)), ((), ())), preferred_element_type=jnp.float32
    )
    raw = jnp.concatenate([raw[:1, s * cells : (s + 1) * cells] for s in range(stations)], axis=0)
    softplus = jnp.maximum(raw, 0.0) + jnp.log1p(jnp.exp(-jnp.abs(raw)))
    out_ref[...] = distance * (0.25 + softplus)


def join_kernel(travel_ref, picks_ref, out_ref):
    travel = travel_ref[...]
    for peer in range(out_ref.shape[0]):
        out_ref[peer, 0] = travel
        out_ref[peer, 1] = picks_ref[peer]


def logit_kernel(blocks_ref, logit_ref, stats_ref):
    peers, _, rows, width = blocks_ref.shape
    half = width // 2
    travel = blocks_ref[:, 0].reshape(peers * rows, width)
    picks = blocks_ref[:, 1].reshape(peers * rows, width)
    weight, arrival = picks[:, :half], picks[:, half:]
    weighted = weight * arrival
    sq_sum = jnp.sum(weighted * arrival, axis=0, keepdims=True)
    mean_sum = jnp.sum(weighted, axis=0, keepdims=True)
    total_w = jnp.sum(weight, axis=0, keepdims=True)
    left = jnp.concatenate([travel * travel, travel], axis=1)
    right = jnp.concatenate([weight, weighted], axis=1)
    product = lax.dot_general(
        left, right, (((0,), (0,)), ((), ())), precision=highest, preferred_element_type=jnp.float32
    )
    curv = product[:width, :half] - 2.0 * product[width:, half:]
    lin = product[width:, :half]
    centered = mean_sum - lin
    logit = -0.5 * (sq_sum + curv - centered * centered / total_w)
    peak = jnp.max(logit, axis=0, keepdims=True)
    total = jnp.sum(jnp.exp(logit - peak), axis=0, keepdims=True)
    logit_ref[...] = logit
    stats = jnp.concatenate([peak, total], axis=1)
    for peer in range(stats_ref.shape[0]):
        stats_ref[peer] = stats


def final_kernel(logit_ref, stats_ref, out_ref):
    half = logit_ref.shape[1]
    peaks = stats_ref[:, 0, :half]
    totals = stats_ref[:, 0, half:]
    peak = jnp.max(peaks, axis=0, keepdims=True)
    total = jnp.sum(totals * jnp.exp(peaks - peak), axis=0, keepdims=True)
    out_ref[...] = (logit_ref[...] - peak - jnp.log(total)).T


def per_device(
    cell_index,
    station_xyz,
    w_cell,
    w_station,
    bias_in,
    w_hidden,
    bias_hidden,
    w_out,
    pick_mask,
    arrival,
    quality,
):
    n_cell, n_sta = lax.axis_size("cell"), lax.axis_size("sta")
    events, stations = pick_mask.shape
    cells = cell_index.shape[1]
    f32 = jnp.float32
    packed = pl.pallas_call(
        pack_kernel, out_shape=jax.ShapeDtypeStruct((n_cell, 2, stations, events), f32), name="pack"
    )(pick_mask.T, arrival.T, quality.T)
    picks = lax.all_to_all(packed, "cell", 0, 0)
    picks = picks.reshape(n_sta, stations, events)
    travel = pl.pallas_call(
        travel_kernel,
        out_shape=jax.ShapeDtypeStruct((stations, cells), f32),
        scratch_shapes=[pltpu.VMEM((stations * cells, w_cell.shape[1]), jnp.bfloat16)],
        compiler_params=pltpu.CompilerParams(vmem_limit_bytes=40 << 20),
        name="travel",
    )(
        cell_index,
        station_xyz,
        w_cell,
        w_station,
        bias_in[None],
        w_hidden,
        bias_hidden,
        w_out[None],
    )
    blocks = pl.pallas_call(
        join_kernel,
        out_shape=jax.ShapeDtypeStruct((n_sta, 2, stations, cells), f32),
        name="join",
    )(travel, picks)
    blocks = lax.all_to_all(blocks, "sta", 0, 0)
    logit, stats = pl.pallas_call(
        logit_kernel,
        out_shape=(
            jax.ShapeDtypeStruct((cells, events // 2), f32),
            jax.ShapeDtypeStruct((n_cell, 1, events), f32),
        ),
        compiler_params=pltpu.CompilerParams(vmem_limit_bytes=40 << 20),
        name="logit",
    )(blocks)
    stats = lax.all_to_all(stats, "cell", 0, 0)
    return pl.pallas_call(
        final_kernel, out_shape=jax.ShapeDtypeStruct((events // 2, cells), f32), name="final"
    )(logit, stats)


def solution(mesh):
    in_specs = (
        P(None, "cell"),
        P(None, "sta"),
        P(),
        P(),
        P(),
        P(),
        P(),
        P(),
        P("cell", "sta"),
        P("cell", "sta"),
        P("cell", "sta"),
    )
    return jax.shard_map(
        per_device, mesh=mesh, in_specs=in_specs, out_specs=P("sta", "cell"), check_vma=False
    )
```

time: 424 us -> 64.9 us (0.15)
  the two profiles are of different devices: /device:TPU:6 before, /device:TPU:8 now
where the time goes in v1:
time: 64.9 us; the launch traced here: 64.4 us
  blocking collectives  34.6 us (53%)
  starting transfers between devices  13 us (20%)
  Pallas kernels  7.62 us (12%)
  waiting for transfers between devices  5.37 us (8%)
  local copies, waits for them, and re-layouts  3.75 us (6%)
    all_to_all x1, blocking collectives, per_device(): blocks = lax.all_to_all(blocks, 'sta', 0, 0)  19.9 us
    all_to_all x1, blocking collectives, per_device(): stats = lax.all_to_all(stats, 'cell', 0, 0)  14.7 us
    all_to_all x1, starting transfers between devices, per_device(): picks = lax.all_to_all(packed, 'cell', 0, 0)  13 us
    all_to_all x1, waiting for transfers between devices, per_device(): picks = lax.all_to_all(packed, 'cell', 0, 0)  5.37 us
    unnamed x22, local copies, waits for them, and re-layouts  3.74 us
    pallas_call x1, Pallas kernels, per_device(): pl.pallas_call(travel_kernel, out_shape=jax.ShapeDtypeStruct((stations, c...  2.18 us
    pallas_call x1, Pallas kernels, per_device(): pl.pallas_call(final_kernel, out_shape=jax.ShapeDtypeStruct((events // 2,...  1.64 us
    pallas_call x1, Pallas kernels, per_device(): pl.pallas_call(join_kernel, out_shape=jax.ShapeDtypeStruct((n_sta, 2, sta...  1.63 us
  transfers between devices with their start and end apart: 1, of which 1 were waited for; matrix products, arithmetic and copies ran while one was open for 0% of the time, Pallas kernels for 3%

profile of v1, /device:TPU:8, one launch (start us, length us, event | category | flops | bytes accessed | tf_op | source)
XLA Modules:
  0.0 64.4 jit_solution(16744280558042498062)
XLA Ops:
  0.0 1.4 %pack.1 = f32[16,2,8,128]{3,2,1,0:T(8,128)} custom-call(s32[8,128]{1,0:T(8,128)} %bitcast.7, f32[8,128]{1,0:T(8,128)} %bitcast.8, f32[8,128]{1,0:T(8,128)} %bitcast.9), custom_call_target="tpu_custom_call" | custom-call | tf_op jit(solution)/shard_map/pack/pallas_call | solution.py:131
  1.4 0.0 copy-start.10
  1.4 0.0 copy-start.3
  1.5 0.0 copy-start.4
  1.5 0.0 copy-start.6
  1.5 0.0 copy-start.7
  1.5 0.0 copy-start.8
  1.5 13.0 %all-to-all-start = ((f32[16,2,8,128]{3,2,1,0:T(8,128)}), f32[16,2,8,128]{3,2,1,0:T(8,128)S(1)}, u32[]{:S(2)}, u32[]{:S(2)}) async-start(f32[16,2,8,128]{3,2,1,0:T(8,128)} %pack.1), calls=%async_computation | async-start | bytes 262144 | tf_op jit(solution)/shard_map/all_to_all | solution.py:134
  14.5 0.0 copy-done.10
  14.5 0.0 copy-start.5
  14.6 0.0 copy-done.3
  14.6 0.0 copy-done.4
  14.6 0.0 copy-done.6
  14.6 0.0 copy-done.7
  14.6 0.0 copy-done.8
  14.6 0.6 copy-done.5
  15.2 0.0 copy-start
  15.2 1.2 %copy-done = bf16[2,512,512]{2,1,0:T(8,128)(2,1)S(1)} copy-done((bf16[2,512,512]{2,1,0:T(8,128)(2,1)S(1)}, bf16[2,512,512]{2,1,0:T(8,128)(2,1)}, u32[]{:S(2)}) %copy-start) | copy-done | bytes 1048600
  16.4 2.2 %travel.1.travel_ref = f32[8,128]{1,0:T(8,128)S(1)} custom-call(s32[3,128]{1,0:T(4,128)S(1)} %copy-done.6, f32[3,8]{1,0:T(4,128)S(1)} %copy-done.7, f32[3,512]{1,0:T(4,128)S(1)} %copy-done.3, f32[3,512]{1,0:T(4,128)S(1)} %copy-done.4, f32[1,512]{1,0:T(1,128)S(1)} %bitcast.5, bf16[2,512,512]{2,1,0:T(8,128)(2,1)S(1)} %copy-done, f32[2,512]{1,0:T(2,128)S(1)} %copy-done.5, ...), custom_call_target="tpu_custom_call" | custom-call | tf_op jit(solution)/shard_map/travel/pallas_call | solution.py:136
  18.6 0.0 copy-start.2
  18.6 0.6 copy-done.2
  19.2 5.4 %all-to-all-done = f32[16,2,8,128]{3,2,1,0:T(8,128)S(1)} async-done(((f32[16,2,8,128]{3,2,1,0:T(8,128)}), f32[16,2,8,128]{3,2,1,0:T(8,128)S(1)}, u32[]{:S(2)}, u32[]{:S(2)}) %all-to-all-start) | async-done | bytes 131104 | tf_op jit(solution)/shard_map/all_to_all | solution.py:134
  24.6 0.0 copy-start.9
  24.6 0.6 %copy-done.9 = f32[16,2,8,128]{3,2,1,0:T(8,128)} copy-done((f32[16,2,8,128]{3,2,1,0:T(8,128)}, f32[16,2,8,128]{3,2,1,0:T(8,128)S(1)}, u32[]{:S(2)}) %copy-start.9) | copy-done | bytes 131096
  25.2 1.6 %join.1 = f32[32,2,8,128]{3,2,1,0:T(8,128)} custom-call(f32[8,128]{1,0:T(8,128)} %copy-done.2, f32[32,8,128]{2,1,0:T(8,128)} %bitcast.6), custom_call_target="tpu_custom_call" | custom-call | tf_op jit(solution)/shard_map/join/pallas_call | solution.py:152
  26.9 19.9 %all_to_all.15.blocks_ref = f32[32,2,8,128]{3,2,1,0:T(8,128)S(1)} all-to-all(f32[32,2,8,128]{3,2,1,0:T(8,128)} %join.1), channel_id=1, replica_groups=mesh['cell'=16,'sta'=32] {'sta'}, dimensions={0} | all-to-all | bytes 524288 | tf_op jit(solution)/shard_map/all_to_all | solution.py:157
  46.7 0.7 %logit.1 = (f32[128,64]{1,0:T(8,128)S(1)}, f32[16,1,128]{2,1,0:T(1,128)S(1)}) custom-call(f32[32,2,8,128]{3,2,1,0:T(8,128)S(1)} %all_to_all.15.blocks_ref), custom_call_target="tpu_custom_call" | custom-call | tf_op jit(solution)/shard_map/logit/pallas_call | solution.py:158
  47.5 0.0 copy-start.1
  47.5 0.6 copy-done.1
  48.1 14.7 %all_to_all.16.stats_ref = f32[16,1,128]{2,1,0:T(1,128)} all-to-all(f32[16,1,128]{2,1,0:T(1,128)S(1)} %get-tuple-element.8), channel_id=1, replica_groups=mesh['cell'=16,'sta'=32] {'cell'}, dimensions={0} | all-to-all | bytes 16384 | tf_op jit(solution)/shard_map/all_to_all | solution.py:167
  62.8 1.6 %final.1 = f32[64,128]{1,0:T(8,128)} custom-call(f32[128,64]{1,0:T(8,128)} %copy-done.1, f32[16,1,128]{2,1,0:T(1,128)} %all_to_all.16.stats_ref), custom_call_target="tpu_custom_call" | custom-call | tf_op jit(solution)/shard_map/final/pallas_call | solution.py:168
  (1 shorter events, 0.0 us)
Async XLA Ops:
  1.4 13.1 %copy-start.10 = (bf16[512]{0:T(512)(128)(2,1)S(1)}, bf16[512]{0:T(512)(128)(2,1)}, u32[]{:S(2)}) copy-start(bf16[512]{0:T(512)(128)(2,1)} %param.18) | copy-start | bytes 3076
  1.4 13.1 %copy-start.3 = (f32[3,512]{1,0:T(4,128)S(1)}, f32[3,512]{1,0:T(4,128)}, u32[]{:S(2)}) copy-start(f32[3,512]{1,0:T(4,128)} %w_cell_ref.1) | copy-start | bytes 18436
  1.5 13.1 %copy-start.4 = (f32[3,512]{1,0:T(4,128)S(1)}, f32[3,512]{1,0:T(4,128)}, u32[]{:S(2)}) copy-start(f32[3,512]{1,0:T(4,128)} %w_station_ref.1) | copy-start | bytes 18436
  1.5 13.1 %copy-start.6 = (s32[3,128]{1,0:T(4,128)S(1)}, s32[3,128]{1,0:T(4,128)}, u32[]{:S(2)}) copy-start(s32[3,128]{1,0:T(4,128)} %cell_ref.1) | copy-start | bytes 4612
  1.5 13.1 %copy-start.7 = (f32[3,8]{1,0:T(4,128)S(1)}, f32[3,8]{1,0:T(4,128)}, u32[]{:S(2)}) copy-start(f32[3,8]{1,0:T(4,128)} %station_ref.1) | copy-start | bytes 292
  1.5 13.1 %copy-start.8 = (f32[512]{0:T(512)S(1)}, f32[512]{0:T(512)}, u32[]{:S(2)}) copy-start(f32[512]{0:T(512)} %param.15) | copy-start | bytes 6148
  1.5 23.1 %all-to-all-start = ((f32[16,2,8,128]{3,2,1,0:T(8,128)}), f32[16,2,8,128]{3,2,1,0:T(8,128)S(1)}, u32[]{:S(2)}, u32[]{:S(2)}) async-start(f32[16,2,8,128]{3,2,1,0:T(8,128)} %pack.1), calls=%async_computation | async-start | bytes 262144 | tf_op jit(solution)/shard_map/all_to_all | solution.py:134
  14.5 0.7 %copy-start.5 = (f32[2,512]{1,0:T(2,128)S(1)}, f32[2,512]{1,0:T(2,128)}, u32[]{:S(2)}) copy-start(f32[2,512]{1,0:T(2,128)} %bias_hidden_ref.1) | copy-start | bytes 12292
  15.2 1.2 %copy-start = (bf16[2,512,512]{2,1,0:T(8,128)(2,1)S(1)}, bf16[2,512,512]{2,1,0:T(8,128)(2,1)}, u32[]{:S(2)}) copy-start(bf16[2,512,512]{2,1,0:T(8,128)(2,1)} %w_hidden_ref.1) | copy-start | bytes 3145732
  18.6 0.6 copy-start.2
  24.6 0.7 %copy-start.9 = (f32[16,2,8,128]{3,2,1,0:T(8,128)}, f32[16,2,8,128]{3,2,1,0:T(8,128)S(1)}, u32[]{:S(2)}) copy-start(f32[16,2,8,128]{3,2,1,0:T(8,128)S(1)} %all-to-all-done) | copy-start | bytes 393220
  47.5 0.6 copy-start.1

commit v2 on v1

--- a/solution.py
+++ b/solution.py
@@ -13,7 +13,13 @@
     return jnp.where(x > 0.0, x, jnp.exp(jnp.minimum(x, 0.0)) - 1.0)
 
 
-def pack_kernel(mask_ref, arrival_ref, quality_ref, out_ref):
+def pack_kernel(mask_hbm, arrival_hbm, quality_hbm, out_ref, mask_ref, arrival_ref, quality_ref, sems):
+    pairs = ((mask_hbm, mask_ref), (arrival_hbm, arrival_ref), (quality_hbm, quality_ref))
+    copies = [pltpu.make_async_copy(*pair, sems.at[k]) for k, pair in enumerate(pairs)]
+    for copy in copies:
+        copy.start()
+    for copy in copies:
+        copy.wait()
     weight = mask_ref[...].astype(jnp.float32) * quality_ref[...]
     arrival = arrival_ref[...]
     half = weight.shape[1] // 2
@@ -30,12 +36,21 @@
     w_cell_ref,
     w_station_ref,
     bias_in_ref,
-    w_hidden_ref,
+    w_hidden_hbm,
     bias_hidden_ref,
     w_out_ref,
     out_ref,
+    w_hidden_ref,
     hidden_ref,
+    sems,
 ):
+    layers = w_hidden_ref.shape[0]
+    copies = [
+        pltpu.make_async_copy(w_hidden_hbm.at[layer], w_hidden_ref.at[layer], sems.at[layer])
+        for layer in range(layers)
+    ]
+    for copy in copies:
+        copy.start()
     stations = station_ref.shape[1]
     cells = cell_ref.shape[1]
     cell = cell_ref[...].astype(jnp.float32) * grid_step
@@ -55,7 +70,8 @@
             jnp.bfloat16
         )
     hidden = hidden_ref[...]
-    for layer in range(w_hidden_ref.shape[0]):
+    for layer in range(layers):
+        copies[layer].wait()
         hidden = elu(
             jnp.dot(hidden, w_hidden_ref[layer], preferred_element_type=jnp.float32)
             + bias_hidden_ref[layer : layer + 1, :]
@@ -109,6 +125,26 @@
     peak = jnp.max(peaks, axis=0, keepdims=True)
     total = jnp.sum(totals * jnp.exp(peaks - peak), axis=0, keepdims=True)
     out_ref[...] = (logit_ref[...] - peak - jnp.log(total)).T
+
+
+vmem = pl.BlockSpec(memory_space=pltpu.VMEM)
+hbm = pl.BlockSpec(memory_space=pltpu.HBM)
+
+
+def in_hbm(x):
+    return pltpu.with_memory_space_constraint(x, pltpu.HBM)
+
+
+def call(kernel, in_specs, out_shape, name, scratch_shapes=()):
+    return pl.pallas_call(
+        kernel,
+        in_specs=in_specs,
+        out_specs=jax.tree.map(lambda _: vmem, out_shape),
+        out_shape=out_shape,
+        scratch_shapes=scratch_shapes,
+        compiler_params=pltpu.CompilerParams(vmem_limit_bytes=40 << 20),
+        name=name,
+    )
 
 
 def per_device(
@@ -128,46 +164,50 @@
     events, stations = pick_mask.shape
     cells = cell_index.shape[1]
     f32 = jnp.float32
-    packed = pl.pallas_call(
-        pack_kernel, out_shape=jax.ShapeDtypeStruct((n_cell, 2, stations, events), f32), name="pack"
-    )(pick_mask.T, arrival.T, quality.T)
-    picks = lax.all_to_all(packed, "cell", 0, 0)
-    picks = picks.reshape(n_sta, stations, events)
-    travel = pl.pallas_call(
+    shape = jax.ShapeDtypeStruct
+    packed = call(
+        pack_kernel,
+        [hbm] * 3,
+        shape((n_cell, 2, stations, events), f32),
+        "pack",
+        [
+            pltpu.VMEM((stations, events), pick_mask.dtype),
+            pltpu.VMEM((stations, events), f32),
+            pltpu.VMEM((stations, events), f32),
+            pltpu.SemaphoreType.DMA((3,)),
+        ],
+    )(*[in_hbm(x.T) for x in (pick_mask, arrival, quality)])
+    picks = lax.all_to_all(packed, "cell", 0, 0).reshape(n_sta, stations, events)
+    travel = call(
         travel_kernel,
-        out_shape=jax.ShapeDtypeStruct((stations, cells), f32),
-        scratch_shapes=[pltpu.VMEM((stations * cells, w_cell.shape[1]), jnp.bfloat16)],
-        compiler_params=pltpu.CompilerParams(vmem_limit_bytes=40 << 20),
-        name="travel",
+        [vmem] * 5 + [hbm] + [vmem] * 2,
+        shape((stations, cells), f32),
+        "travel",
+        [
+            pltpu.VMEM(w_hidden.shape, w_hidden.dtype),
+            pltpu.VMEM((stations * cells, w_cell.shape[1]), jnp.bfloat16),
+            pltpu.SemaphoreType.DMA((w_hidden.shape[0],)),
+        ],
     )(
         cell_index,
         station_xyz,
         w_cell,
         w_station,
         bias_in[None],
-        w_hidden,
+        in_hbm(w_hidden),
         bias_hidden,
         w_out[None],
     )
-    blocks = pl.pallas_call(
-        join_kernel,
-        out_shape=jax.ShapeDtypeStruct((n_sta, 2, stations, cells), f32),
-        name="join",
-    )(travel, picks)
+    blocks = call(join_kernel, [vmem] * 2, shape((n_sta, 2, stations, cells), f32), "join")(travel, picks)
     blocks = lax.all_to_all(blocks, "sta", 0, 0)
-    logit, stats = pl.pallas_call(
+    logit, stats = call(
         logit_kernel,
-        out_shape=(
-            jax.ShapeDtypeStruct((cells, events // 2), f32),
-            jax.ShapeDtypeStruct((n_cell, 1, events), f32),
-        ),
-        compiler_params=pltpu.CompilerParams(vmem_limit_bytes=40 << 20),
-        name="logit",
+        [vmem],
+        (shape((cells, events // 2), f32), shape((n_cell, 1, events), f32)),
+        "logit",
     )(blocks)
     stats = lax.all_to_all(stats, "cell", 0, 0)
-    return pl.pallas_call(
-        final_kernel, out_shape=jax.ShapeDtypeStruct((events // 2, cells), f32), name="final"
-    )(logit, stats)
+    return call(final_kernel, [vmem] * 2, shape((events // 2, cells), f32), "final")(logit, stats)
 
 
 def solution(mesh):

time: 64.9 us -> 60.1 us (0.926)
  local copies, waits for them, and re-layouts: 3.75 us -> 0.66 us
  Pallas kernels: 7.62 us -> 6.23 us
  blocking collectives: 34.6 us -> 33.5 us
  waiting for transfers between devices: 5.37 us -> 6.15 us
    unnamed x22 -> x14, local copies, waits for them, and re-layouts: 3.74 us -> 0.66 us
    pallas_call x5, Pallas kernels: 7.62 us -> 6.23 us  [the longest x1 3.22 us: per_device(): call(travel_kernel, [vmem] * 5 + [hbm] + [vmem] * 2, shape((stations, cel...]
    all_to_all x1, blocking collectives: 14.7 us -> 13.8 us  [per_device(): stats = lax.all_to_all(stats, 'cell', 0, 0)]
    all_to_all x1, waiting for transfers between devices: 5.37 us -> 6.15 us  [per_device(): lax.all_to_all(packed, 'cell', 0, 0).reshape(n_sta, stations, events)]
  transfers between devices with their start and end apart: 1 -> 1, of which waited for: 1 -> 1; matrix products, arithmetic and copies ran while one was open for 0% -> 0% of each run, Pallas kernels for 3% -> 5%
where the time goes in v2:
time: 60.1 us; the launch traced here: 59.7 us
  blocking collectives  33.5 us (56%)
  starting transfers between devices  13 us (22%)
  Pallas kernels  6.23 us (10%)
  waiting for transfers between devices  6.15 us (10%)
  local copies, waits for them, and re-layouts  0.66 us (1%)
    all_to_all x1, blocking collectives, per_device(): blocks = lax.all_to_all(blocks, 'sta', 0, 0)  19.7 us
    all_to_all x1, blocking collectives, per_device(): stats = lax.all_to_all(stats, 'cell', 0, 0)  13.8 us
    all_to_all x1, starting transfers between devices, per_device(): lax.all_to_all(packed, 'cell', 0, 0).reshape(n_sta, stations, events)  13 us
    all_to_all x1, waiting for transfers between devices, per_device(): lax.all_to_all(packed, 'cell', 0, 0).reshape(n_sta, stations, events)  6.15 us
    pallas_call x1, Pallas kernels, per_device(): call(travel_kernel, [vmem] * 5 + [hbm] + [vmem] * 2, shape((stations, cel...  3.22 us
    pallas_call x1, Pallas kernels, per_device(): call(pack_kernel, [hbm] * 3, shape((n_cell, 2, stations, events), f32), '...  1.46 us
  transfers between devices with their start and end apart: 1, of which 1 were waited for; matrix products, arithmetic and copies ran while one was open for 0% of the time, Pallas kernels for 5%

profile of v2, /device:TPU:8, one launch (start us, length us, event | category | flops | bytes accessed | tf_op | source)
XLA Modules:
  0.0 59.7 jit_solution(5870978571891448272)
XLA Ops:
  0.0 1.5 %pack.1 = f32[16,2,8,128]{3,2,1,0:T(8,128)} custom-call(s32[8,128]{1,0:T(8,128)} %bitcast.7, f32[8,128]{1,0:T(8,128)} %bitcast.8, f32[8,128]{1,0:T(8,128)} %bitcast.9), custom_call_target="tpu_custom_call" | custom-call | tf_op jit(solution)/shard_map/pack/pallas_call | solution.py:168
  1.5 0.0 copy-start.6
  1.5 0.0 copy-start
  1.5 0.0 copy-start.1
  1.5 0.0 copy-start.3
  1.5 0.0 copy-start.4
  1.5 0.0 copy-start.5
  1.5 13.0 %all-to-all-start = ((f32[16,2,8,128]{3,2,1,0:T(8,128)}), f32[16,2,8,128]{3,2,1,0:T(8,128)S(1)}, u32[]{:S(2)}, u32[]{:S(2)}) async-start(f32[16,2,8,128]{3,2,1,0:T(8,128)} %pack.1), calls=%async_computation | async-start | bytes 262144 | tf_op jit(solution)/shard_map/all_to_all | solution.py:180
  14.6 0.0 copy-done.6
  14.6 0.0 copy-start.2
  14.6 0.0 copy-done
  14.6 0.0 copy-done.1
  14.6 0.0 copy-done.3
  14.6 0.0 copy-done.4
  14.7 0.0 copy-done.5
  14.7 0.6 %copy-done.2 = f32[2,512]{1,0:T(2,128)S(1)} copy-done((f32[2,512]{1,0:T(2,128)S(1)}, f32[2,512]{1,0:T(2,128)}, u32[]{:S(2)}) %copy-start.2) | copy-done | bytes 4120
  15.3 3.2 %travel.1.travel_ref = f32[8,128]{1,0:T(8,128)S(1)} custom-call(s32[3,128]{1,0:T(4,128)S(1)} %copy-done.3, f32[3,8]{1,0:T(4,128)S(1)} %copy-done.4, f32[3,512]{1,0:T(4,128)S(1)} %copy-done, f32[3,512]{1,0:T(4,128)S(1)} %copy-done.1, f32[1,512]{1,0:T(1,128)S(1)} %bitcast.6, bf16[2,512,512]{2,1,0:T(8,128)(2,1)} %w_hidden_hbm.1, f32[2,512]{1,0:T(2,128)S(1)} %copy-done.2, ...), custom_call_target="tpu_custom_call" | custom-call | tf_op jit(solution)/shard_map/travel/pallas_call | solution.py:181
  18.5 6.1 %all-to-all-done = f32[16,2,8,128]{3,2,1,0:T(8,128)S(1)} async-done(((f32[16,2,8,128]{3,2,1,0:T(8,128)}), f32[16,2,8,128]{3,2,1,0:T(8,128)S(1)}, u32[]{:S(2)}, u32[]{:S(2)}) %all-to-all-start) | async-done | bytes 131104 | tf_op jit(solution)/shard_map/all_to_all | solution.py:180
  24.7 19.7 %all_to_all.15.blocks_ref = f32[32,2,8,128]{3,2,1,0:T(8,128)S(1)} all-to-all(f32[32,2,8,128]{3,2,1,0:T(8,128)S(1)} %join.1), channel_id=1, replica_groups=mesh['cell'=16,'sta'=32] {'sta'}, dimensions={0} | all-to-all | bytes 524288 | tf_op jit(solution)/shard_map/all_to_all | solution.py:202
  44.4 0.7 %logit.1 = (f32[128,64]{1,0:T(8,128)S(1)}, f32[16,1,128]{2,1,0:T(1,128)S(1)}) custom-call(f32[32,2,8,128]{3,2,1,0:T(8,128)S(1)} %all_to_all.15.blocks_ref), custom_call_target="tpu_custom_call" | custom-call | tf_op jit(solution)/shard_map/logit/pallas_call | solution.py:203
  45.1 13.8 %all_to_all.16.stats_ref = f32[16,1,128]{2,1,0:T(1,128)S(1)} all-to-all(f32[16,1,128]{2,1,0:T(1,128)S(1)} %get-tuple-element.8), channel_id=1, replica_groups=mesh['cell'=16,'sta'=32] {'cell'}, dimensions={0} | all-to-all | bytes 16384 | tf_op jit(solution)/shard_map/all_to_all | solution.py:209
  58.9 0.8 %final.1 = f32[64,128]{1,0:T(8,128)} custom-call(f32[128,64]{1,0:T(8,128)S(1)} %get-tuple-element.7.logit_ref, f32[16,1,128]{2,1,0:T(1,128)S(1)} %all_to_all.16.stats_ref), custom_call_target="tpu_custom_call" | custom-call | tf_op jit(solution)/shard_map/final/pallas_call | solution.py:210
  (2 shorter events, 0.0 us)
Async XLA Ops:
  1.5 13.1 %copy-start.6 = (bf16[512]{0:T(512)(128)(2,1)S(1)}, bf16[512]{0:T(512)(128)(2,1)}, u32[]{:S(2)}) copy-start(bf16[512]{0:T(512)(128)(2,1)} %param.18) | copy-start | bytes 3076
  1.5 13.1 %copy-start = (f32[3,512]{1,0:T(4,128)S(1)}, f32[3,512]{1,0:T(4,128)}, u32[]{:S(2)}) copy-start(f32[3,512]{1,0:T(4,128)} %w_cell_ref.1) | copy-start | bytes 18436
  1.5 13.1 %copy-start.1 = (f32[3,512]{1,0:T(4,128)S(1)}, f32[3,512]{1,0:T(4,128)}, u32[]{:S(2)}) copy-start(f32[3,512]{1,0:T(4,128)} %w_station_ref.1) | copy-start | bytes 18436
  1.5 13.1 %copy-start.3 = (s32[3,128]{1,0:T(4,128)S(1)}, s32[3,128]{1,0:T(4,128)}, u32[]{:S(2)}) copy-start(s32[3,128]{1,0:T(4,128)} %cell_ref.1) | copy-start | bytes 4612
  1.5 13.1 %copy-start.4 = (f32[3,8]{1,0:T(4,128)S(1)}, f32[3,8]{1,0:T(4,128)}, u32[]{:S(2)}) copy-start(f32[3,8]{1,0:T(4,128)} %station_ref.1) | copy-start | bytes 292
  1.5 13.1 %copy-start.5 = (f32[512]{0:T(512)S(1)}, f32[512]{0:T(512)}, u32[]{:S(2)}) copy-start(f32[512]{0:T(512)} %param.15) | copy-start | bytes 6148
  1.5 23.1 %all-to-all-start = ((f32[16,2,8,128]{3,2,1,0:T(8,128)}), f32[16,2,8,128]{3,2,1,0:T(8,128)S(1)}, u32[]{:S(2)}, u32[]{:S(2)}) async-start(f32[16,2,8,128]{3,2,1,0:T(8,128)} %pack.1), calls=%async_computation | async-start | bytes 262144 | tf_op jit(solution)/shard_map/all_to_all | solution.py:180
  14.6 0.7 %copy-start.2 = (f32[2,512]{1,0:T(2,128)S(1)}, f32[2,512]{1,0:T(2,128)}, u32[]{:S(2)}) copy-start(f32[2,512]{1,0:T(2,128)} %bias_hidden_ref.1) | copy-start | bytes 12292

commit v3 on v2

--- a/solution.py
+++ b/solution.py
@@ -88,14 +88,16 @@
     travel = travel_ref[...]
     for peer in range(out_ref.shape[0]):
         out_ref[peer, 0] = travel
-        out_ref[peer, 1] = picks_ref[peer]
+        for h in range(2):
+            out_ref[peer, 1 + h] = picks_ref[peer, h]
 
 
 def logit_kernel(blocks_ref, logit_ref, stats_ref):
-    peers, _, rows, width = blocks_ref.shape
+    cores, peers, _, rows, width = blocks_ref.shape
     half = width // 2
-    travel = blocks_ref[:, 0].reshape(peers * rows, width)
-    picks = blocks_ref[:, 1].reshape(peers * rows, width)
+    odd = lax.axis_index("sta") % 2 == 1
+    travel = blocks_ref[:, :, 0].reshape(cores * peers * rows, width)
+    picks = jnp.where(odd, blocks_ref[:, :, 2], blocks_ref[:, :, 1]).reshape(cores * peers * rows, width)
     weight, arrival = picks[:, :half], picks[:, half:]
     weighted = weight * arrival
     sq_sum = jnp.sum(weighted * arrival, axis=0, keepdims=True)
@@ -177,7 +179,7 @@
             pltpu.SemaphoreType.DMA((3,)),
         ],
     )(*[in_hbm(x.T) for x in (pick_mask, arrival, quality)])
-    picks = lax.all_to_all(packed, "cell", 0, 0).reshape(n_sta, stations, events)
+    picks = lax.all_to_all(packed, "cell", 0, 0)
     travel = call(
         travel_kernel,
         [vmem] * 5 + [hbm] + [vmem] * 2,
@@ -198,8 +200,11 @@
         bias_hidden,
         w_out[None],
     )
-    blocks = call(join_kernel, [vmem] * 2, shape((n_sta, 2, stations, cells), f32), "join")(travel, picks)
-    blocks = lax.all_to_all(blocks, "sta", 0, 0)
+    blocks = call(join_kernel, [vmem] * 2, shape((n_cell, 3, stations, cells), f32), "join")(travel, picks)
+    equal_cores = [list(range(core, n_sta, 2)) for core in range(2)]
+    pairs = [[chip, chip + 1] for chip in range(0, n_sta, 2)]
+    blocks = lax.all_to_all(blocks, "sta", 0, 0, axis_index_groups=equal_cores)
+    blocks = lax.all_gather(blocks, "sta", axis_index_groups=pairs)
     logit, stats = call(
         logit_kernel,
         [vmem],

time: 60.1 us -> 58.5 us (0.973)
  blocking collectives: 33.5 us -> 31.9 us
    all_to_all x1, blocking collectives: 19.7 us -> 15.9 us  [per_device(): blocks = lax.all_to_all(blocks, 'sta', 0, 0, axis_index_groups=equal_cores)]
    all_gather x0 -> x1, blocking collectives: none -> 2.08 us  [per_device(): blocks = lax.all_gather(blocks, 'sta', axis_index_groups=pairs)]
  transfers between devices with their start and end apart: 1 -> 1, of which waited for: 1 -> 1; matrix products, arithmetic and copies ran while one was open for 0% -> 0% of each run, Pallas kernels for 5% -> 6%
where the time goes in v3:
time: 58.5 us; the launch traced here: 58.1 us
  blocking collectives  31.9 us (55%)
  starting transfers between devices  13 us (22%)
  Pallas kernels  6.24 us (11%)
  waiting for transfers between devices  6.15 us (11%)
  local copies, waits for them, and re-layouts  0.66 us (1%)
    all_to_all x1, blocking collectives, per_device(): blocks = lax.all_to_all(blocks, 'sta', 0, 0, axis_index_groups=equal_cores)  15.9 us
    all_to_all x1, blocking collectives, per_device(): stats = lax.all_to_all(stats, 'cell', 0, 0)  14 us
    all_to_all x1, starting transfers between devices, per_device(): picks = lax.all_to_all(packed, 'cell', 0, 0)  13 us
    all_to_all x1, waiting for transfers between devices, per_device(): picks = lax.all_to_all(packed, 'cell', 0, 0)  6.15 us
    pallas_call x1, Pallas kernels, per_device(): call(travel_kernel, [vmem] * 5 + [hbm] + [vmem] * 2, shape((stations, cel...  3.22 us
    all_gather x1, blocking collectives, per_device(): blocks = lax.all_gather(blocks, 'sta', axis_index_groups=pairs)  2.08 us
    pallas_call x1, Pallas kernels, per_device(): call(pack_kernel, [hbm] * 3, shape((n_cell, 2, stations, events), f32), '...  1.46 us
  transfers between devices with their start and end apart: 1, of which 1 were waited for; matrix products, arithmetic and copies ran while one was open for 0% of the time, Pallas kernels for 6%

profile of v3, /device:TPU:8, one launch (start us, length us, event | category | flops | bytes accessed | tf_op | source)
XLA Modules:
  0.0 58.1 jit_solution(8351045495513945976)
XLA Ops:
  0.0 1.5 %pack.1 = f32[16,2,8,128]{3,2,1,0:T(8,128)} custom-call(s32[8,128]{1,0:T(8,128)} %bitcast.7, f32[8,128]{1,0:T(8,128)} %bitcast.8, f32[8,128]{1,0:T(8,128)} %bitcast.9), custom_call_target="tpu_custom_call" | custom-call | tf_op jit(solution)/shard_map/pack/pallas_call | solution.py:170
  1.5 0.0 copy-start.6
  1.5 0.0 copy-start
  1.5 0.0 copy-start.1
  1.5 0.0 copy-start.3
  1.5 0.0 copy-start.4
  1.5 0.0 copy-start.5
  1.5 13.0 %all-to-all-start = ((f32[16,2,8,128]{3,2,1,0:T(8,128)}), f32[16,2,8,128]{3,2,1,0:T(8,128)S(1)}, u32[]{:S(2)}, u32[]{:S(2)}) async-start(f32[16,2,8,128]{3,2,1,0:T(8,128)} %pack.1), calls=%async_computation | async-start | bytes 262144 | tf_op jit(solution)/shard_map/all_to_all | solution.py:182
  14.6 0.0 copy-done.6
  14.6 0.0 copy-start.2
  14.6 0.0 copy-done
  14.6 0.0 copy-done.1
  14.6 0.0 copy-done.3
  14.6 0.0 copy-done.4
  14.7 0.0 copy-done.5
  14.7 0.6 %copy-done.2 = f32[2,512]{1,0:T(2,128)S(1)} copy-done((f32[2,512]{1,0:T(2,128)S(1)}, f32[2,512]{1,0:T(2,128)}, u32[]{:S(2)}) %copy-start.2) | copy-done | bytes 4120
  15.3 3.2 %travel.1.travel_ref = f32[8,128]{1,0:T(8,128)S(1)} custom-call(s32[3,128]{1,0:T(4,128)S(1)} %copy-done.3, f32[3,8]{1,0:T(4,128)S(1)} %copy-done.4, f32[3,512]{1,0:T(4,128)S(1)} %copy-done, f32[3,512]{1,0:T(4,128)S(1)} %copy-done.1, f32[1,512]{1,0:T(1,128)S(1)} %bitcast.6, bf16[2,512,512]{2,1,0:T(8,128)(2,1)} %w_hidden_hbm.1, f32[2,512]{1,0:T(2,128)S(1)} %copy-done.2, ...), custom_call_target="tpu_custom_call" | custom-call | tf_op jit(solution)/shard_map/travel/pallas_call | solution.py:183
  18.5 6.1 %all-to-all-done.picks_ref = f32[16,2,8,128]{3,2,1,0:T(8,128)S(1)} async-done(((f32[16,2,8,128]{3,2,1,0:T(8,128)}), f32[16,2,8,128]{3,2,1,0:T(8,128)S(1)}, u32[]{:S(2)}, u32[]{:S(2)}) %all-to-all-start) | async-done | bytes 131104 | tf_op jit(solution)/shard_map/all_to_all | solution.py:182
  24.7 15.9 %all_to_all.15 = f32[16,3,8,128]{3,2,1,0:T(8,128)S(1)} all-to-all(f32[16,3,8,128]{3,2,1,0:T(8,128)S(1)} %join.1), channel_id=1, replica_groups={{0,2,4,6,8,10,12,14,16,18,20,22,24,26,28,30},{1,3,5,7,9,11,13,15,17,19,..., dimensions={0} | all-to-all | bytes 393216 | tf_op jit(solution)/shard_map/all_to_all | solution.py:206
  40.6 2.1 %all-gather = f32[32,3,8,128]{3,2,1,0:T(8,128)S(1)} all-gather(f32[16,3,8,128]{3,2,1,0:T(8,128)S(1)} %all_to_all.15), channel_id=2, replica_groups={{0,1},{2,3},{4,5},{6,7},{8,9},{10,11},{12,13},{14,15},{16,17},{18,19},{..., dimensions={0}, use_global_device_ids=true | all-gather | bytes 589824 | tf_op jit(solution)/shard_map/all_gather | solution.py:207
  42.6 0.7 %logit.1 = (f32[128,64]{1,0:T(8,128)S(1)}, f32[16,1,128]{2,1,0:T(1,128)S(1)}) custom-call(f32[2,16,3,8,128]{4,3,2,1,0:T(8,128)S(1)} %bitcast.5), custom_call_target="tpu_custom_call" | custom-call | tf_op jit(solution)/shard_map/logit/pallas_call | solution.py:208
  43.4 14.0 %all_to_all.16.stats_ref = f32[16,1,128]{2,1,0:T(1,128)S(1)} all-to-all(f32[16,1,128]{2,1,0:T(1,128)S(1)} %get-tuple-element.8), channel_id=1, replica_groups=mesh['cell'=16,'sta'=32] {'cell'}, dimensions={0} | all-to-all | bytes 16384 | tf_op jit(solution)/shard_map/all_to_all | solution.py:214
  57.3 0.8 %final.1 = f32[64,128]{1,0:T(8,128)} custom-call(f32[128,64]{1,0:T(8,128)S(1)} %get-tuple-element.7.logit_ref, f32[16,1,128]{2,1,0:T(1,128)S(1)} %all_to_all.16.stats_ref), custom_call_target="tpu_custom_call" | custom-call | tf_op jit(solution)/shard_map/final/pallas_call | solution.py:215
  (2 shorter events, 0.0 us)
Async XLA Ops:
  1.5 13.1 %copy-start.6 = (bf16[512]{0:T(512)(128)(2,1)S(1)}, bf16[512]{0:T(512)(128)(2,1)}, u32[]{:S(2)}) copy-start(bf16[512]{0:T(512)(128)(2,1)} %param.18) | copy-start | bytes 3076
  1.5 13.1 %copy-start = (f32[3,512]{1,0:T(4,128)S(1)}, f32[3,512]{1,0:T(4,128)}, u32[]{:S(2)}) copy-start(f32[3,512]{1,0:T(4,128)} %w_cell_ref.1) | copy-start | bytes 18436
  1.5 13.1 %copy-start.1 = (f32[3,512]{1,0:T(4,128)S(1)}, f32[3,512]{1,0:T(4,128)}, u32[]{:S(2)}) copy-start(f32[3,512]{1,0:T(4,128)} %w_station_ref.1) | copy-start | bytes 18436
  1.5 13.1 %copy-start.3 = (s32[3,128]{1,0:T(4,128)S(1)}, s32[3,128]{1,0:T(4,128)}, u32[]{:S(2)}) copy-start(s32[3,128]{1,0:T(4,128)} %cell_ref.1) | copy-start | bytes 4612
  1.5 13.1 %copy-start.4 = (f32[3,8]{1,0:T(4,128)S(1)}, f32[3,8]{1,0:T(4,128)}, u32[]{:S(2)}) copy-start(f32[3,8]{1,0:T(4,128)} %station_ref.1) | copy-start | bytes 292
  1.5 13.1 %copy-start.5 = (f32[512]{0:T(512)S(1)}, f32[512]{0:T(512)}, u32[]{:S(2)}) copy-start(f32[512]{0:T(512)} %param.15) | copy-start | bytes 6148
  1.5 23.1 %all-to-all-start = ((f32[16,2,8,128]{3,2,1,0:T(8,128)}), f32[16,2,8,128]{3,2,1,0:T(8,128)S(1)}, u32[]{:S(2)}, u32[]{:S(2)}) async-start(f32[16,2,8,128]{3,2,1,0:T(8,128)} %pack.1), calls=%async_computation | async-start | bytes 262144 | tf_op jit(solution)/shard_map/all_to_all | solution.py:182
  14.6 0.7 %copy-start.2 = (f32[2,512]{1,0:T(2,128)S(1)}, f32[2,512]{1,0:T(2,128)}, u32[]{:S(2)}) copy-start(f32[2,512]{1,0:T(2,128)} %bias_hidden_ref.1) | copy-start | bytes 12292

commit v4 on v3

--- a/solution.py
+++ b/solution.py
@@ -22,12 +22,9 @@
         copy.wait()
     weight = mask_ref[...].astype(jnp.float32) * quality_ref[...]
     arrival = arrival_ref[...]
-    half = weight.shape[1] // 2
-    for h in range(2):
-        part = slice(h * half, (h + 1) * half)
-        block = jnp.concatenate([weight[:, part], arrival[:, part]], axis=1)
-        for peer in range(out_ref.shape[0]):
-            out_ref[peer, h] = block
+    for peer in range(out_ref.shape[0]):
+        out_ref[peer, 0] = weight
+        out_ref[peer, 1] = arrival
 
 
 def travel_kernel(
@@ -36,21 +33,16 @@
     w_cell_ref,
     w_station_ref,
     bias_in_ref,
-    w_hidden_hbm,
-    bias_hidden_ref,
+    w_hidden_ref,
+    bias_hidden_hbm,
     w_out_ref,
     out_ref,
-    w_hidden_ref,
     hidden_ref,
-    sems,
+    bias_hidden_ref,
+    sem,
 ):
-    layers = w_hidden_ref.shape[0]
-    copies = [
-        pltpu.make_async_copy(w_hidden_hbm.at[layer], w_hidden_ref.at[layer], sems.at[layer])
-        for layer in range(layers)
-    ]
-    for copy in copies:
-        copy.start()
+    bias_copy = pltpu.make_async_copy(bias_hidden_hbm, bias_hidden_ref, sem)
+    bias_copy.start()
     stations = station_ref.shape[1]
     cells = cell_ref.shape[1]
     cell = cell_ref[...].astype(jnp.float32) * grid_step
@@ -70,8 +62,8 @@
             jnp.bfloat16
         )
     hidden = hidden_ref[...]
-    for layer in range(layers):
-        copies[layer].wait()
+    bias_copy.wait()
+    for layer in range(w_hidden_ref.shape[0]):
         hidden = elu(
             jnp.dot(hidden, w_hidden_ref[layer], preferred_element_type=jnp.float32)
             + bias_hidden_ref[layer : layer + 1, :]
@@ -88,8 +80,8 @@
     travel = travel_ref[...]
     for peer in range(out_ref.shape[0]):
         out_ref[peer, 0] = travel
-        for h in range(2):
-            out_ref[peer, 1 + h] = picks_ref[peer, h]
+        for k in range(2):
+            out_ref[peer, 1 + k] = picks_ref[peer, k]
 
 
 def logit_kernel(blocks_ref, logit_ref, stats_ref):
@@ -97,8 +89,10 @@
     half = width // 2
     odd = lax.axis_index("sta") % 2 == 1
     travel = blocks_ref[:, :, 0].reshape(cores * peers * rows, width)
-    picks = jnp.where(odd, blocks_ref[:, :, 2], blocks_ref[:, :, 1]).reshape(cores * peers * rows, width)
-    weight, arrival = picks[:, :half], picks[:, half:]
+    weight, arrival = [
+        jnp.where(odd, member[:, half:], member[:, :half])
+        for member in [blocks_ref[:, :, k].reshape(cores * peers * rows, width) for k in (1, 2)]
+    ]
     weighted = weight * arrival
     sq_sum = jnp.sum(weighted * arrival, axis=0, keepdims=True)
     mean_sum = jnp.sum(weighted, axis=0, keepdims=True)
@@ -137,7 +131,7 @@
     return pltpu.with_memory_space_constraint(x, pltpu.HBM)
 
 
-def call(kernel, in_specs, out_shape, name, scratch_shapes=()):
+def call(kernel, in_specs, out_shape, name, scratch_shapes=(), cost=None):
     return pl.pallas_call(
         kernel,
         in_specs=in_specs,
@@ -146,6 +140,7 @@
         scratch_shapes=scratch_shapes,
         compiler_params=pltpu.CompilerParams(vmem_limit_bytes=40 << 20),
         name=name,
+        cost_estimate=cost,
     )
 
 
@@ -178,17 +173,18 @@
             pltpu.VMEM((stations, events), f32),
             pltpu.SemaphoreType.DMA((3,)),
         ],
+        pl.CostEstimate(flops=2 * 10**9, transcendentals=0, bytes_accessed=10**6),
     )(*[in_hbm(x.T) for x in (pick_mask, arrival, quality)])
     picks = lax.all_to_all(packed, "cell", 0, 0)
     travel = call(
         travel_kernel,
-        [vmem] * 5 + [hbm] + [vmem] * 2,
+        [vmem] * 6 + [hbm, vmem],
         shape((stations, cells), f32),
         "travel",
         [
-            pltpu.VMEM(w_hidden.shape, w_hidden.dtype),
             pltpu.VMEM((stations * cells, w_cell.shape[1]), jnp.bfloat16),
-            pltpu.SemaphoreType.DMA((w_hidden.shape[0],)),
+            pltpu.VMEM(bias_hidden.shape, f32),
+            pltpu.SemaphoreType.DMA,
         ],
     )(
         cell_index,
@@ -196,8 +192,8 @@
         w_cell,
         w_station,
         bias_in[None],
-        in_hbm(w_hidden),
-        bias_hidden,
+        w_hidden,
+        in_hbm(bias_hidden),
         w_out[None],
     )
     blocks = call(join_kernel, [vmem] * 2, shape((n_cell, 3, stations, cells), f32), "join")(travel, picks)

time: 58.5 us -> 58.2 us (level)
  transfers between devices with their start and end apart: 1 -> 1, of which waited for: 1 -> 1; matrix products, arithmetic and copies ran while one was open for 0% -> 0% of each run, Pallas kernels for 6% -> 5%
where the time goes in v4:
time: 58.2 us; the launch traced here: 57.8 us
  blocking collectives  31.6 us (54%)
  starting transfers between devices  13 us (22%)
  waiting for transfers between devices  6.7 us (12%)
  Pallas kernels  5.73 us (10%)
  local copies, waits for them, and re-layouts  0.67 us (1%)
    all_to_all x1, blocking collectives, per_device(): blocks = lax.all_to_all(blocks, 'sta', 0, 0, axis_index_groups=equal_cores)  15.9 us
    all_to_all x1, blocking collectives, per_device(): stats = lax.all_to_all(stats, 'cell', 0, 0)  13.6 us
    all_to_all x1, starting transfers between devices, per_device(): picks = lax.all_to_all(packed, 'cell', 0, 0)  13 us
    all_to_all x1, waiting for transfers between devices, per_device(): picks = lax.all_to_all(packed, 'cell', 0, 0)  6.7 us
    pallas_call x1, Pallas kernels, per_device(): call(travel_kernel, [vmem] * 6 + [hbm, vmem], shape((stations, cells), f3...  2.66 us
    all_gather x1, blocking collectives, per_device(): blocks = lax.all_gather(blocks, 'sta', axis_index_groups=pairs)  2.08 us
    pallas_call x1, Pallas kernels, per_device(): call(pack_kernel, [hbm] * 3, shape((n_cell, 2, stations, events), f32), '...  1.49 us
  transfers between devices with their start and end apart: 1, of which 1 were waited for; matrix products, arithmetic and copies ran while one was open for 0% of the time, Pallas kernels for 5%

profile of v4, /device:TPU:8, one launch (start us, length us, event | category | flops | bytes accessed | tf_op | source)
XLA Modules:
  0.0 57.8 jit_solution(13577785479455425074)
XLA Ops:
  0.0 0.0 copy-start
  0.0 1.5 %pack.1 = f32[16,2,8,128]{3,2,1,0:T(8,128)} custom-call(s32[8,128]{1,0:T(8,128)} %bitcast.7, f32[8,128]{1,0:T(8,128)} %bitcast.8, f32[8,128]{1,0:T(8,128)} %bitcast.9), custom_call_target="tpu_custom_call" | custom-call | flops 2000000000 | bytes 1000000 | tf_op jit(solution)/shard_map/pack/pallas_call | solution.py:165
  1.5 0.0 copy-start.6
  1.5 0.0 copy-start.1
  1.5 0.0 copy-start.2
  1.5 0.0 copy-start.5
  1.5 13.0 %all-to-all-start = ((f32[16,2,8,128]{3,2,1,0:T(8,128)}), f32[16,2,8,128]{3,2,1,0:T(8,128)S(1)}, u32[]{:S(2)}, u32[]{:S(2)}) async-start(f32[16,2,8,128]{3,2,1,0:T(8,128)} %pack.1), calls=%async_computation | async-start | bytes 262144 | tf_op jit(solution)/shard_map/all_to_all | solution.py:178
  14.6 0.0 copy-done.6
  14.6 0.0 copy-start.3
  14.6 0.0 copy-start.4
  14.6 0.0 copy-done
  14.6 0.0 copy-done.1
  14.6 0.0 copy-done.2
  14.7 0.0 copy-done.5
  14.7 0.6 %copy-done.3 = s32[3,128]{1,0:T(4,128)S(1)} copy-done((s32[3,128]{1,0:T(4,128)S(1)}, s32[3,128]{1,0:T(4,128)}, u32[]{:S(2)}) %copy-start.3) | copy-done | bytes 1560
  15.3 0.0 copy-done.4
  15.3 2.7 %travel.1.travel_ref = f32[8,128]{1,0:T(8,128)S(1)} custom-call(s32[3,128]{1,0:T(4,128)S(1)} %copy-done.3, f32[3,8]{1,0:T(4,128)S(1)} %copy-done.4, f32[3,512]{1,0:T(4,128)S(1)} %copy-done.1, f32[3,512]{1,0:T(4,128)S(1)} %copy-done.2, f32[1,512]{1,0:T(1,128)S(1)} %bitcast.6, bf16[2,512,512]{2,1,0:T(8,128)(2,1)S(1)} %copy-done, f32[2,512]{1,0:T(2,128)} %bias_hidden_hbm.1, ...), custom_call_target="tpu_custom_call" | custom-call | tf_op jit(solution)/shard_map/travel/pallas_call | solution.py:179
  18.0 6.7 %all-to-all-done.picks_ref = f32[16,2,8,128]{3,2,1,0:T(8,128)S(1)} async-done(((f32[16,2,8,128]{3,2,1,0:T(8,128)}), f32[16,2,8,128]{3,2,1,0:T(8,128)S(1)}, u32[]{:S(2)}, u32[]{:S(2)}) %all-to-all-start) | async-done | bytes 131104 | tf_op jit(solution)/shard_map/all_to_all | solution.py:178
  24.7 15.9 %all_to_all.15 = f32[16,3,8,128]{3,2,1,0:T(8,128)S(1)} all-to-all(f32[16,3,8,128]{3,2,1,0:T(8,128)S(1)} %join.1), channel_id=1, replica_groups={{0,2,4,6,8,10,12,14,16,18,20,22,24,26,28,30},{1,3,5,7,9,11,13,15,17,19,..., dimensions={0} | all-to-all | bytes 393216 | tf_op jit(solution)/shard_map/all_to_all | solution.py:202
  40.6 2.1 %all-gather = f32[32,3,8,128]{3,2,1,0:T(8,128)S(1)} all-gather(f32[16,3,8,128]{3,2,1,0:T(8,128)S(1)} %all_to_all.15), channel_id=2, replica_groups={{0,1},{2,3},{4,5},{6,7},{8,9},{10,11},{12,13},{14,15},{16,17},{18,19},{..., dimensions={0}, use_global_device_ids=true | all-gather | bytes 589824 | tf_op jit(solution)/shard_map/all_gather | solution.py:203
  42.6 0.8 %logit.1 = (f32[128,64]{1,0:T(8,128)S(1)}, f32[16,1,128]{2,1,0:T(1,128)S(1)}) custom-call(f32[2,16,3,8,128]{4,3,2,1,0:T(8,128)S(1)} %bitcast.5), custom_call_target="tpu_custom_call" | custom-call | tf_op jit(solution)/shard_map/logit/pallas_call | solution.py:204
  43.4 13.6 %all_to_all.16.stats_ref = f32[16,1,128]{2,1,0:T(1,128)S(1)} all-to-all(f32[16,1,128]{2,1,0:T(1,128)S(1)} %get-tuple-element.8), channel_id=1, replica_groups=mesh['cell'=16,'sta'=32] {'cell'}, dimensions={0} | all-to-all | bytes 16384 | tf_op jit(solution)/shard_map/all_to_all | solution.py:210
  57.0 0.8 %final.1 = f32[64,128]{1,0:T(8,128)} custom-call(f32[128,64]{1,0:T(8,128)S(1)} %get-tuple-element.7.logit_ref, f32[16,1,128]{2,1,0:T(1,128)S(1)} %all_to_all.16.stats_ref), custom_call_target="tpu_custom_call" | custom-call | tf_op jit(solution)/shard_map/final/pallas_call | solution.py:211
  (2 shorter events, 0.0 us)
Async XLA Ops:
  0.0 14.6 %copy-start = (bf16[2,512,512]{2,1,0:T(8,128)(2,1)S(1)}, bf16[2,512,512]{2,1,0:T(8,128)(2,1)}, u32[]{:S(2)}) copy-start(bf16[2,512,512]{2,1,0:T(8,128)(2,1)} %w_hidden_ref.1) | copy-start | bytes 3145732
  1.5 13.1 %copy-start.6 = (bf16[512]{0:T(512)(128)(2,1)S(1)}, bf16[512]{0:T(512)(128)(2,1)}, u32[]{:S(2)}) copy-start(bf16[512]{0:T(512)(128)(2,1)} %param.18) | copy-start | bytes 3076
  1.5 13.1 %copy-start.1 = (f32[3,512]{1,0:T(4,128)S(1)}, f32[3,512]{1,0:T(4,128)}, u32[]{:S(2)}) copy-start(f32[3,512]{1,0:T(4,128)} %w_cell_ref.1) | copy-start | bytes 18436
  1.5 13.1 %copy-start.2 = (f32[3,512]{1,0:T(4,128)S(1)}, f32[3,512]{1,0:T(4,128)}, u32[]{:S(2)}) copy-start(f32[3,512]{1,0:T(4,128)} %w_station_ref.1) | copy-start | bytes 18436
  1.5 13.1 %copy-start.5 = (f32[512]{0:T(512)S(1)}, f32[512]{0:T(512)}, u32[]{:S(2)}) copy-start(f32[512]{0:T(512)} %param.15) | copy-start | bytes 6148
  1.5 23.1 %all-to-all-start = ((f32[16,2,8,128]{3,2,1,0:T(8,128)}), f32[16,2,8,128]{3,2,1,0:T(8,128)S(1)}, u32[]{:S(2)}, u32[]{:S(2)}) async-start(f32[16,2,8,128]{3,2,1,0:T(8,128)} %pack.1), calls=%async_computation | async-start | bytes 262144 | tf_op jit(solution)/shard_map/all_to_all | solution.py:178
  14.6 0.7 %copy-start.3 = (s32[3,128]{1,0:T(4,128)S(1)}, s32[3,128]{1,0:T(4,128)}, u32[]{:S(2)}) copy-start(s32[3,128]{1,0:T(4,128)} %cell_ref.1) | copy-start | bytes 4612
  14.6 0.7 %copy-start.4 = (f32[3,8]{1,0:T(4,128)S(1)}, f32[3,8]{1,0:T(4,128)}, u32[]{:S(2)}) copy-start(f32[3,8]{1,0:T(4,128)} %station_ref.1) | copy-start | bytes 292

commit v5 on v4

--- a/solution.py
+++ b/solution.py
@@ -88,39 +88,44 @@
     cores, peers, _, rows, width = blocks_ref.shape
     half = width // 2
     odd = lax.axis_index("sta") % 2 == 1
-    travel = blocks_ref[:, :, 0].reshape(cores * peers * rows, width)
+    travel, weight, arrival = [
+        blocks_ref[:, :, k].reshape(cores * peers * rows, width) for k in range(3)
+    ]
     weight, arrival = [
-        jnp.where(odd, member[:, half:], member[:, :half])
-        for member in [blocks_ref[:, :, k].reshape(cores * peers * rows, width) for k in (1, 2)]
+        jnp.where(odd, member[half:], member[:half]) for member in (weight.T, arrival.T)
     ]
     weighted = weight * arrival
-    sq_sum = jnp.sum(weighted * arrival, axis=0, keepdims=True)
-    mean_sum = jnp.sum(weighted, axis=0, keepdims=True)
-    total_w = jnp.sum(weight, axis=0, keepdims=True)
-    left = jnp.concatenate([travel * travel, travel], axis=1)
-    right = jnp.concatenate([weight, weighted], axis=1)
-    product = lax.dot_general(
-        left, right, (((0,), (0,)), ((), ())), precision=highest, preferred_element_type=jnp.float32
-    )
-    curv = product[:width, :half] - 2.0 * product[width:, half:]
-    lin = product[width:, :half]
-    centered = mean_sum - lin
+    sq_sum = jnp.sum(weighted * arrival, axis=1, keepdims=True)
+    mean_sum = jnp.sum(weighted, axis=1, keepdims=True)
+    total_w = jnp.sum(weight, axis=1, keepdims=True)
+    product = jnp.dot(
+        jnp.concatenate([weight, weighted], axis=0),
+        jnp.concatenate([travel * travel, travel], axis=1),
+        precision=highest,
+        preferred_element_type=jnp.float32,
+    )
+    curv = product[:half, :width] - 2.0 * product[half:, width:]
+    centered = mean_sum - product[:half, width:]
     logit = -0.5 * (sq_sum + curv - centered * centered / total_w)
-    peak = jnp.max(logit, axis=0, keepdims=True)
-    total = jnp.sum(jnp.exp(logit - peak), axis=0, keepdims=True)
+    peak = jnp.max(logit, axis=1, keepdims=True)
+    total = jnp.sum(jnp.exp(logit - peak), axis=1, keepdims=True)
     logit_ref[...] = logit
-    stats = jnp.concatenate([peak, total], axis=1)
+    lane = lax.broadcasted_iota(jnp.int32, logit.shape, 1)
+    rows = jnp.where(lane == 0, peak, total).T
+    stats = jnp.concatenate([rows[:1], rows[1:2]], axis=1)
     for peer in range(stats_ref.shape[0]):
         stats_ref[peer] = stats
 
 
 def final_kernel(logit_ref, stats_ref, out_ref):
-    half = logit_ref.shape[1]
+    half = logit_ref.shape[0]
     peaks = stats_ref[:, 0, :half]
     totals = stats_ref[:, 0, half:]
     peak = jnp.max(peaks, axis=0, keepdims=True)
     total = jnp.sum(totals * jnp.exp(peaks - peak), axis=0, keepdims=True)
-    out_ref[...] = (logit_ref[...] - peak - jnp.log(total)).T
+    row = lax.broadcasted_iota(jnp.int32, (8, peaks.shape[1]), 0)
+    columns = jnp.where(row == 0, peak, jnp.log(total)).T
+    out_ref[...] = logit_ref[...] - columns[:, :1] - columns[:, 1:2]
 
 
 vmem = pl.BlockSpec(memory_space=pltpu.VMEM)
@@ -204,7 +209,7 @@
     logit, stats = call(
         logit_kernel,
         [vmem],
-        (shape((cells, events // 2), f32), shape((n_cell, 1, events), f32)),
+        (shape((events // 2, cells), f32), shape((n_cell, 1, events), f32)),
         "logit",
     )(blocks)
     stats = lax.all_to_all(stats, "cell", 0, 0)

time: 58.2 us -> 58.1 us (level)
  no operation moved by 1% of the time
where the time goes in v5:
time: 58.1 us; the launch traced here: 57.8 us
  blocking collectives  31.6 us (54%)
  starting transfers between devices  13 us (22%)
  waiting for transfers between devices  6.7 us (12%)
  Pallas kernels  5.68 us (10%)
  local copies, waits for them, and re-layouts  0.67 us (1%)
    all_to_all x1, blocking collectives, per_device(): blocks = lax.all_to_all(blocks, 'sta', 0, 0, axis_index_groups=equal_cores)  15.9 us
    all_to_all x1, blocking collectives, per_device(): stats = lax.all_to_all(stats, 'cell', 0, 0)  13.6 us
    all_to_all x1, starting transfers between devices, per_device(): picks = lax.all_to_all(packed, 'cell', 0, 0)  13 us
    all_to_all x1, waiting for transfers between devices, per_device(): picks = lax.all_to_all(packed, 'cell', 0, 0)  6.7 us
    pallas_call x1, Pallas kernels, per_device(): call(travel_kernel, [vmem] * 6 + [hbm, vmem], shape((stations, cells), f3...  2.66 us
    all_gather x1, blocking collectives, per_device(): blocks = lax.all_gather(blocks, 'sta', axis_index_groups=pairs)  2.08 us
    pallas_call x1, Pallas kernels, per_device(): call(pack_kernel, [hbm] * 3, shape((n_cell, 2, stations, events), f32), '...  1.49 us
  transfers between devices with their start and end apart: 1, of which 1 were waited for; matrix products, arithmetic and copies ran while one was open for 0% of the time, Pallas kernels for 5%

profile of v5, /device:TPU:8, one launch (start us, length us, event | category | flops | bytes accessed | tf_op | source)
XLA Modules:
  0.0 57.8 jit_solution(11789284538348781623)
XLA Ops:
  0.0 0.0 copy-start
  0.0 1.5 %pack.1 = f32[16,2,8,128]{3,2,1,0:T(8,128)} custom-call(s32[8,128]{1,0:T(8,128)} %bitcast.7, f32[8,128]{1,0:T(8,128)} %bitcast.8, f32[8,128]{1,0:T(8,128)} %bitcast.9), custom_call_target="tpu_custom_call" | custom-call | flops 2000000000 | bytes 1000000 | tf_op jit(solution)/shard_map/pack/pallas_call | solution.py:170
  1.5 0.0 copy-start.6
  1.5 0.0 copy-start.1
  1.5 0.0 copy-start.2
  1.5 0.0 copy-start.5
  1.5 13.0 %all-to-all-start = ((f32[16,2,8,128]{3,2,1,0:T(8,128)}), f32[16,2,8,128]{3,2,1,0:T(8,128)S(1)}, u32[]{:S(2)}, u32[]{:S(2)}) async-start(f32[16,2,8,128]{3,2,1,0:T(8,128)} %pack.1), calls=%async_computation | async-start | bytes 262144 | tf_op jit(solution)/shard_map/all_to_all | solution.py:183
  14.6 0.0 copy-done.6
  14.6 0.0 copy-start.3
  14.6 0.0 copy-start.4
  14.6 0.0 copy-done
  14.6 0.0 copy-done.1
  14.6 0.0 copy-done.2
  14.7 0.0 copy-done.5
  14.7 0.6 %copy-done.3 = s32[3,128]{1,0:T(4,128)S(1)} copy-done((s32[3,128]{1,0:T(4,128)S(1)}, s32[3,128]{1,0:T(4,128)}, u32[]{:S(2)}) %copy-start.3) | copy-done | bytes 1560
  15.3 0.0 copy-done.4
  15.3 2.7 %travel.1.travel_ref = f32[8,128]{1,0:T(8,128)S(1)} custom-call(s32[3,128]{1,0:T(4,128)S(1)} %copy-done.3, f32[3,8]{1,0:T(4,128)S(1)} %copy-done.4, f32[3,512]{1,0:T(4,128)S(1)} %copy-done.1, f32[3,512]{1,0:T(4,128)S(1)} %copy-done.2, f32[1,512]{1,0:T(1,128)S(1)} %bitcast.6, bf16[2,512,512]{2,1,0:T(8,128)(2,1)S(1)} %copy-done, f32[2,512]{1,0:T(2,128)} %bias_hidden_hbm.1, ...), custom_call_target="tpu_custom_call" | custom-call | tf_op jit(solution)/shard_map/travel/pallas_call | solution.py:184
  18.0 6.7 %all-to-all-done.picks_ref = f32[16,2,8,128]{3,2,1,0:T(8,128)S(1)} async-done(((f32[16,2,8,128]{3,2,1,0:T(8,128)}), f32[16,2,8,128]{3,2,1,0:T(8,128)S(1)}, u32[]{:S(2)}, u32[]{:S(2)}) %all-to-all-start) | async-done | bytes 131104 | tf_op jit(solution)/shard_map/all_to_all | solution.py:183
  24.7 15.9 %all_to_all.15 = f32[16,3,8,128]{3,2,1,0:T(8,128)S(1)} all-to-all(f32[16,3,8,128]{3,2,1,0:T(8,128)S(1)} %join.1), channel_id=1, replica_groups={{0,2,4,6,8,10,12,14,16,18,20,22,24,26,28,30},{1,3,5,7,9,11,13,15,17,19,..., dimensions={0} | all-to-all | bytes 393216 | tf_op jit(solution)/shard_map/all_to_all | solution.py:207
  40.6 2.1 %all-gather = f32[32,3,8,128]{3,2,1,0:T(8,128)S(1)} all-gather(f32[16,3,8,128]{3,2,1,0:T(8,128)S(1)} %all_to_all.15), channel_id=2, replica_groups={{0,1},{2,3},{4,5},{6,7},{8,9},{10,11},{12,13},{14,15},{16,17},{18,19},{..., dimensions={0}, use_global_device_ids=true | all-gather | bytes 589824 | tf_op jit(solution)/shard_map/all_gather | solution.py:208
  42.6 0.6 %logit.1 = (f32[64,128]{1,0:T(8,128)S(1)}, f32[16,1,128]{2,1,0:T(1,128)S(1)}) custom-call(f32[2,16,3,8,128]{4,3,2,1,0:T(8,128)S(1)} %bitcast.5), custom_call_target="tpu_custom_call" | custom-call | tf_op jit(solution)/shard_map/logit/pallas_call | solution.py:209
  43.3 13.6 %all_to_all.16.stats_ref = f32[16,1,128]{2,1,0:T(1,128)S(1)} all-to-all(f32[16,1,128]{2,1,0:T(1,128)S(1)} %get-tuple-element.8), channel_id=1, replica_groups=mesh['cell'=16,'sta'=32] {'cell'}, dimensions={0} | all-to-all | bytes 16384 | tf_op jit(solution)/shard_map/all_to_all | solution.py:215
  56.9 0.9 %final.1 = f32[64,128]{1,0:T(8,128)} custom-call(f32[64,128]{1,0:T(8,128)S(1)} %get-tuple-element.7.logit_ref, f32[16,1,128]{2,1,0:T(1,128)S(1)} %all_to_all.16.stats_ref), custom_call_target="tpu_custom_call" | custom-call | tf_op jit(solution)/shard_map/final/pallas_call | solution.py:216
  (2 shorter events, 0.0 us)
Async XLA Ops:
  0.0 14.6 %copy-start = (bf16[2,512,512]{2,1,0:T(8,128)(2,1)S(1)}, bf16[2,512,512]{2,1,0:T(8,128)(2,1)}, u32[]{:S(2)}) copy-start(bf16[2,512,512]{2,1,0:T(8,128)(2,1)} %w_hidden_ref.1) | copy-start | bytes 3145732
  1.5 13.1 %copy-start.6 = (bf16[512]{0:T(512)(128)(2,1)S(1)}, bf16[512]{0:T(512)(128)(2,1)}, u32[]{:S(2)}) copy-start(bf16[512]{0:T(512)(128)(2,1)} %param.18) | copy-start | bytes 3076
  1.5 13.1 %copy-start.1 = (f32[3,512]{1,0:T(4,128)S(1)}, f32[3,512]{1,0:T(4,128)}, u32[]{:S(2)}) copy-start(f32[3,512]{1,0:T(4,128)} %w_cell_ref.1) | copy-start | bytes 18436
  1.5 13.1 %copy-start.2 = (f32[3,512]{1,0:T(4,128)S(1)}, f32[3,512]{1,0:T(4,128)}, u32[]{:S(2)}) copy-start(f32[3,512]{1,0:T(4,128)} %w_station_ref.1) | copy-start | bytes 18436
  1.5 13.1 %copy-start.5 = (f32[512]{0:T(512)S(1)}, f32[512]{0:T(512)}, u32[]{:S(2)}) copy-start(f32[512]{0:T(512)} %param.15) | copy-start | bytes 6148
  1.5 23.1 %all-to-all-start = ((f32[16,2,8,128]{3,2,1,0:T(8,128)}), f32[16,2,8,128]{3,2,1,0:T(8,128)S(1)}, u32[]{:S(2)}, u32[]{:S(2)}) async-start(f32[16,2,8,128]{3,2,1,0:T(8,128)} %pack.1), calls=%async_computation | async-start | bytes 262144 | tf_op jit(solution)/shard_map/all_to_all | solution.py:183
  14.6 0.7 %copy-start.3 = (s32[3,128]{1,0:T(4,128)S(1)}, s32[3,128]{1,0:T(4,128)}, u32[]{:S(2)}) copy-start(s32[3,128]{1,0:T(4,128)} %cell_ref.1) | copy-start | bytes 4612
  14.6 0.7 %copy-start.4 = (f32[3,8]{1,0:T(4,128)S(1)}, f32[3,8]{1,0:T(4,128)}, u32[]{:S(2)}) copy-start(f32[3,8]{1,0:T(4,128)} %station_ref.1) | copy-start | bytes 292

commit v6 on v5

--- a/solution.py
+++ b/solution.py
@@ -6,6 +6,8 @@
 from jax.sharding import PartitionSpec as P
 
 grid_step = 0.015625
+first_picks, first_blocks, first_stats = 12, 12, 12
+pair_order = (0, 1)
 highest = lax.Precision.HIGHEST
 
 
@@ -76,12 +78,17 @@
     out_ref[...] = distance * (0.25 + softplus)
 
 
+def rotated(count, first):
+    return [(first + place) % count for place in range(count)]
+
+
 def join_kernel(travel_ref, picks_ref, out_ref):
     travel = travel_ref[...]
-    for peer in range(out_ref.shape[0]):
-        out_ref[peer, 0] = travel
+    peers = out_ref.shape[0]
+    for place, chip in enumerate(rotated(peers, first_blocks)):
+        out_ref[place, 0] = travel
         for k in range(2):
-            out_ref[peer, 1 + k] = picks_ref[peer, k]
+            out_ref[place, 1 + k] = picks_ref[rotated(peers, first_picks).index(chip), k]
 
 
 def logit_kernel(blocks_ref, logit_ref, stats_ref):
@@ -180,7 +187,7 @@
         ],
         pl.CostEstimate(flops=2 * 10**9, transcendentals=0, bytes_accessed=10**6),
     )(*[in_hbm(x.T) for x in (pick_mask, arrival, quality)])
-    picks = lax.all_to_all(packed, "cell", 0, 0)
+    picks = lax.all_to_all(packed, "cell", 0, 0, axis_index_groups=[rotated(n_cell, first_picks)])
     travel = call(
         travel_kernel,
         [vmem] * 6 + [hbm, vmem],
@@ -202,8 +209,8 @@
         w_out[None],
     )
     blocks = call(join_kernel, [vmem] * 2, shape((n_cell, 3, stations, cells), f32), "join")(travel, picks)
-    equal_cores = [list(range(core, n_sta, 2)) for core in range(2)]
-    pairs = [[chip, chip + 1] for chip in range(0, n_sta, 2)]
+    equal_cores = [[2 * chip + core for chip in rotated(n_cell, first_blocks)] for core in range(2)]
+    pairs = [[2 * chip + core for core in pair_order] for chip in range(n_cell)]
     blocks = lax.all_to_all(blocks, "sta", 0, 0, axis_index_groups=equal_cores)
     blocks = lax.all_gather(blocks, "sta", axis_index_groups=pairs)
     logit, stats = call(
@@ -212,7 +219,7 @@
         (shape((events // 2, cells), f32), shape((n_cell, 1, events), f32)),
         "logit",
     )(blocks)
-    stats = lax.all_to_all(stats, "cell", 0, 0)
+    stats = lax.all_to_all(stats, "cell", 0, 0, axis_index_groups=[rotated(n_cell, first_stats)])
     return call(final_kernel, [vmem] * 2, shape((events // 2, cells), f32), "final")(logit, stats)
 
 

time: 58.1 us -> 51.7 us (0.89)
  the two profiles are of different devices: /device:TPU:8 before, /device:TPU:6 now
where the time goes in v6:
time: 51.7 us; the launch traced here: 51.4 us
  blocking collectives  27.6 us (53%)
  starting transfers between devices  14.6 us (28%)
  Pallas kernels  5.68 us (11%)
  waiting for transfers between devices  2.74 us (5%)
  local copies, waits for them, and re-layouts  0.67 us (1%)
    all_to_all x1, starting transfers between devices, per_device(): lax.all_to_all(packed, 'cell', 0, 0, axis_index_groups=[rotated(n_cell, f...  14.6 us
    all_to_all x1, blocking collectives, per_device(): blocks = lax.all_to_all(blocks, 'sta', 0, 0, axis_index_groups=equal_cores)  13.5 us
    all_to_all x1, blocking collectives, per_device(): lax.all_to_all(stats, 'cell', 0, 0, axis_index_groups=[rotated(n_cell, fi...  12.1 us
    all_to_all x1, waiting for transfers between devices, per_device(): lax.all_to_all(packed, 'cell', 0, 0, axis_index_groups=[rotated(n_cell, f...  2.74 us
    pallas_call x1, Pallas kernels, per_device(): call(travel_kernel, [vmem] * 6 + [hbm, vmem], shape((stations, cells), f3...  2.66 us
    all_gather x1, blocking collectives, per_device(): blocks = lax.all_gather(blocks, 'sta', axis_index_groups=pairs)  2.08 us
    pallas_call x1, Pallas kernels, per_device(): call(pack_kernel, [hbm] * 3, shape((n_cell, 2, stations, events), f32), '...  1.49 us
  transfers between devices with their start and end apart: 1, of which 1 were waited for; matrix products, arithmetic and copies ran while one was open for 0% of the time, Pallas kernels for 5%

profile of v6, /device:TPU:6, one launch (start us, length us, event | category | flops | bytes accessed | tf_op | source)
XLA Modules:
  0.0 51.4 jit_solution(12753953898745295314)
XLA Ops:
  0.0 0.0 copy-start
  0.0 1.5 %pack.1 = f32[16,2,8,128]{3,2,1,0:T(8,128)} custom-call(s32[8,128]{1,0:T(8,128)} %bitcast.7, f32[8,128]{1,0:T(8,128)} %bitcast.8, f32[8,128]{1,0:T(8,128)} %bitcast.9), custom_call_target="tpu_custom_call" | custom-call | flops 2000000000 | bytes 1000000 | tf_op jit(solution)/shard_map/pack/pallas_call | solution.py:177
  1.5 0.0 copy-start.6
  1.5 0.0 copy-start.1
  1.5 0.0 copy-start.2
  1.5 0.0 copy-start.5
  1.5 14.6 %all-to-all-start = ((f32[16,2,8,128]{3,2,1,0:T(8,128)}), f32[16,2,8,128]{3,2,1,0:T(8,128)S(1)}, u32[]{:S(2)}, u32[]{:S(2)}) async-start(f32[16,2,8,128]{3,2,1,0:T(8,128)} %pack.1), calls=%async_computation | async-start | bytes 262144 | tf_op jit(solution)/shard_map/all_to_all | solution.py:190
  16.1 0.0 copy-done.6
  16.1 0.0 copy-start.3
  16.1 0.0 copy-start.4
  16.2 0.0 copy-done
  16.2 0.0 copy-done.1
  16.2 0.0 copy-done.2
  16.2 0.0 copy-done.5
  16.2 0.6 %copy-done.3 = s32[3,128]{1,0:T(4,128)S(1)} copy-done((s32[3,128]{1,0:T(4,128)S(1)}, s32[3,128]{1,0:T(4,128)}, u32[]{:S(2)}) %copy-start.3) | copy-done | bytes 1560
  16.8 0.0 copy-done.4
  16.8 2.7 %travel.1.travel_ref = f32[8,128]{1,0:T(8,128)S(1)} custom-call(s32[3,128]{1,0:T(4,128)S(1)} %copy-done.3, f32[3,8]{1,0:T(4,128)S(1)} %copy-done.4, f32[3,512]{1,0:T(4,128)S(1)} %copy-done.1, f32[3,512]{1,0:T(4,128)S(1)} %copy-done.2, f32[1,512]{1,0:T(1,128)S(1)} %bitcast.6, bf16[2,512,512]{2,1,0:T(8,128)(2,1)S(1)} %copy-done, f32[2,512]{1,0:T(2,128)} %bias_hidden_hbm.1, ...), custom_call_target="tpu_custom_call" | custom-call | tf_op jit(solution)/shard_map/travel/pallas_call | solution.py:191
  19.5 2.7 %all-to-all-done.picks_ref = f32[16,2,8,128]{3,2,1,0:T(8,128)S(1)} async-done(((f32[16,2,8,128]{3,2,1,0:T(8,128)}), f32[16,2,8,128]{3,2,1,0:T(8,128)S(1)}, u32[]{:S(2)}, u32[]{:S(2)}) %all-to-all-start) | async-done | bytes 131104 | tf_op jit(solution)/shard_map/all_to_all | solution.py:190
  22.3 13.5 %all_to_all.15 = f32[16,3,8,128]{3,2,1,0:T(8,128)S(1)} all-to-all(f32[16,3,8,128]{3,2,1,0:T(8,128)S(1)} %join.1), channel_id=1, replica_groups={{24,26,28,30,0,2,4,6,8,10,12,14,16,18,20,22},{25,27,29,31,1,3,5,7,9,11,..., dimensions={0} | all-to-all | bytes 393216 | tf_op jit(solution)/shard_map/all_to_all | solution.py:214
  35.7 2.1 %all-gather = f32[32,3,8,128]{3,2,1,0:T(8,128)S(1)} all-gather(f32[16,3,8,128]{3,2,1,0:T(8,128)S(1)} %all_to_all.15), channel_id=2, replica_groups={{0,1},{2,3},{4,5},{6,7},{8,9},{10,11},{12,13},{14,15},{16,17},{18,19},{..., dimensions={0}, use_global_device_ids=true | all-gather | bytes 589824 | tf_op jit(solution)/shard_map/all_gather | solution.py:215
  37.8 0.6 %logit.1 = (f32[64,128]{1,0:T(8,128)S(1)}, f32[16,1,128]{2,1,0:T(1,128)S(1)}) custom-call(f32[2,16,3,8,128]{4,3,2,1,0:T(8,128)S(1)} %bitcast.5), custom_call_target="tpu_custom_call" | custom-call | tf_op jit(solution)/shard_map/logit/pallas_call | solution.py:216
  38.4 12.1 %all_to_all.16.stats_ref = f32[16,1,128]{2,1,0:T(1,128)S(1)} all-to-all(f32[16,1,128]{2,1,0:T(1,128)S(1)} %get-tuple-element.8), channel_id=1, replica_groups={{384,416,448,480,0,32,64,96,128,160,192,224,256,288,320,352},{385,417,4..., dimensions={0} | all-to-all | bytes 16384 | tf_op jit(solution)/shard_map/all_to_all | solution.py:222
  50.5 0.9 %final.1 = f32[64,128]{1,0:T(8,128)} custom-call(f32[64,128]{1,0:T(8,128)S(1)} %get-tuple-element.7.logit_ref, f32[16,1,128]{2,1,0:T(1,128)S(1)} %all_to_all.16.stats_ref), custom_call_target="tpu_custom_call" | custom-call | tf_op jit(solution)/shard_map/final/pallas_call | solution.py:223
  (2 shorter events, 0.0 us)
Async XLA Ops:
  0.0 16.2 %copy-start = (bf16[2,512,512]{2,1,0:T(8,128)(2,1)S(1)}, bf16[2,512,512]{2,1,0:T(8,128)(2,1)}, u32[]{:S(2)}) copy-start(bf16[2,512,512]{2,1,0:T(8,128)(2,1)} %w_hidden_ref.1) | copy-start | bytes 3145732
  1.5 14.6 %copy-start.6 = (bf16[512]{0:T(512)(128)(2,1)S(1)}, bf16[512]{0:T(512)(128)(2,1)}, u32[]{:S(2)}) copy-start(bf16[512]{0:T(512)(128)(2,1)} %param.18) | copy-start | bytes 3076
  1.5 14.7 %copy-start.1 = (f32[3,512]{1,0:T(4,128)S(1)}, f32[3,512]{1,0:T(4,128)}, u32[]{:S(2)}) copy-start(f32[3,512]{1,0:T(4,128)} %w_cell_ref.1) | copy-start | bytes 18436
  1.5 14.7 %copy-start.2 = (f32[3,512]{1,0:T(4,128)S(1)}, f32[3,512]{1,0:T(4,128)}, u32[]{:S(2)}) copy-start(f32[3,512]{1,0:T(4,128)} %w_station_ref.1) | copy-start | bytes 18436
  1.5 14.7 %copy-start.5 = (f32[512]{0:T(512)S(1)}, f32[512]{0:T(512)}, u32[]{:S(2)}) copy-start(f32[512]{0:T(512)} %param.15) | copy-start | bytes 6148
  1.5 20.7 %all-to-all-start = ((f32[16,2,8,128]{3,2,1,0:T(8,128)}), f32[16,2,8,128]{3,2,1,0:T(8,128)S(1)}, u32[]{:S(2)}, u32[]{:S(2)}) async-start(f32[16,2,8,128]{3,2,1,0:T(8,128)} %pack.1), calls=%async_computation | async-start | bytes 262144 | tf_op jit(solution)/shard_map/all_to_all | solution.py:190
  16.1 0.7 %copy-start.3 = (s32[3,128]{1,0:T(4,128)S(1)}, s32[3,128]{1,0:T(4,128)}, u32[]{:S(2)}) copy-start(s32[3,128]{1,0:T(4,128)} %cell_ref.1) | copy-start | bytes 4612
  16.1 0.7 %copy-start.4 = (f32[3,8]{1,0:T(4,128)S(1)}, f32[3,8]{1,0:T(4,128)}, u32[]{:S(2)}) copy-start(f32[3,8]{1,0:T(4,128)} %station_ref.1) | copy-start | bytes 292

commit v7 on v6

--- a/solution.py
+++ b/solution.py
@@ -6,17 +6,35 @@
 from jax.sharding import PartitionSpec as P
 
 grid_step = 0.015625
-first_picks, first_blocks, first_stats = 12, 12, 12
-pair_order = (0, 1)
+first_picks, first_blocks, first_stats = 12, 25, 12
 highest = lax.Precision.HIGHEST
 
 
 def elu(x):
-    return jnp.where(x > 0.0, x, jnp.exp(jnp.minimum(x, 0.0)) - 1.0)
-
-
-def pack_kernel(mask_hbm, arrival_hbm, quality_hbm, out_ref, mask_ref, arrival_ref, quality_ref, sems):
-    pairs = ((mask_hbm, mask_ref), (arrival_hbm, arrival_ref), (quality_hbm, quality_ref))
+    return jnp.where(x > 0.0, x, jnp.exp(x) - 1.0)
+
+
+def pack_kernel(
+    mask_hbm,
+    arrival_hbm,
+    quality_hbm,
+    cell_hbm,
+    station_hbm,
+    out_ref,
+    cell_ref,
+    station_ref,
+    mask_ref,
+    arrival_ref,
+    quality_ref,
+    sems,
+):
+    pairs = (
+        (mask_hbm, mask_ref),
+        (arrival_hbm, arrival_ref),
+        (quality_hbm, quality_ref),
+        (cell_hbm, cell_ref),
+        (station_hbm, station_ref),
+    )
     copies = [pltpu.make_async_copy(*pair, sems.at[k]) for k, pair in enumerate(pairs)]
     for copy in copies:
         copy.start()
@@ -36,15 +54,11 @@
     w_station_ref,
     bias_in_ref,
     w_hidden_ref,
-    bias_hidden_hbm,
+    bias_hidden_ref,
     w_out_ref,
     out_ref,
     hidden_ref,
-    bias_hidden_ref,
-    sem,
 ):
-    bias_copy = pltpu.make_async_copy(bias_hidden_hbm, bias_hidden_ref, sem)
-    bias_copy.start()
     stations = station_ref.shape[1]
     cells = cell_ref.shape[1]
     cell = cell_ref[...].astype(jnp.float32) * grid_step
@@ -64,7 +78,6 @@
             jnp.bfloat16
         )
     hidden = hidden_ref[...]
-    bias_copy.wait()
     for layer in range(w_hidden_ref.shape[0]):
         hidden = elu(
             jnp.dot(hidden, w_hidden_ref[layer], preferred_element_type=jnp.float32)
@@ -85,22 +98,24 @@
 def join_kernel(travel_ref, picks_ref, out_ref):
     travel = travel_ref[...]
     peers = out_ref.shape[0]
-    for place, chip in enumerate(rotated(peers, first_blocks)):
+    for place, member in enumerate(rotated(peers, first_blocks)):
+        chip, core = divmod(member, 2)
         out_ref[place, 0] = travel
-        for k in range(2):
-            out_ref[place, 1 + k] = picks_ref[rotated(peers, first_picks).index(chip), k]
+        w = picks_ref[rotated(peers // 2, first_picks).index(chip), 0]
+        a = picks_ref[rotated(peers // 2, first_picks).index(chip), 1]
+        half = w.shape[1] // 2
+        part = slice(core * half, (core + 1) * half)
+        out_ref[place, 1] = jnp.concatenate([w[:, part], a[:, part]], axis=1)
 
 
 def logit_kernel(blocks_ref, logit_ref, stats_ref):
-    cores, peers, _, rows, width = blocks_ref.shape
+    peers, _, rows, width = blocks_ref.shape
     half = width // 2
-    odd = lax.axis_index("sta") % 2 == 1
-    travel, weight, arrival = [
-        blocks_ref[:, :, k].reshape(cores * peers * rows, width) for k in range(3)
+    travel, picks = [
+        blocks_ref[:, k].reshape(peers * rows, width) for k in range(2)
     ]
-    weight, arrival = [
-        jnp.where(odd, member[half:], member[:half]) for member in (weight.T, arrival.T)
-    ]
+    picks = picks.T
+    weight, arrival = picks[:half], picks[half:]
     weighted = weight * arrival
     sq_sum = jnp.sum(weighted * arrival, axis=1, keepdims=True)
     mean_sum = jnp.sum(weighted, axis=1, keepdims=True)
@@ -130,9 +145,8 @@
     totals = stats_ref[:, 0, half:]
     peak = jnp.max(peaks, axis=0, keepdims=True)
     total = jnp.sum(totals * jnp.exp(peaks - peak), axis=0, keepdims=True)
-    row = lax.broadcasted_iota(jnp.int32, (8, peaks.shape[1]), 0)
-    columns = jnp.where(row == 0, peak, jnp.log(total)).T
-    out_ref[...] = logit_ref[...] - columns[:, :1] - columns[:, 1:2]
+    shift = jnp.broadcast_to(peak + jnp.log(total), (8, half)).T
+    out_ref[...] = logit_ref[...] - shift[:, :1]
 
 
 vmem = pl.BlockSpec(memory_space=pltpu.VMEM)
@@ -174,30 +188,30 @@
     cells = cell_index.shape[1]
     f32 = jnp.float32
     shape = jax.ShapeDtypeStruct
-    packed = call(
+    packed, cell_index, station_xyz = call(
         pack_kernel,
-        [hbm] * 3,
-        shape((n_cell, 2, stations, events), f32),
+        [hbm] * 5,
+        (
+            shape((n_cell, 2, stations, events), f32),
+            shape(cell_index.shape, cell_index.dtype),
+            shape(station_xyz.shape, f32),
+        ),
         "pack",
         [
             pltpu.VMEM((stations, events), pick_mask.dtype),
             pltpu.VMEM((stations, events), f32),
             pltpu.VMEM((stations, events), f32),
-            pltpu.SemaphoreType.DMA((3,)),
+            pltpu.SemaphoreType.DMA((5,)),
         ],
         pl.CostEstimate(flops=2 * 10**9, transcendentals=0, bytes_accessed=10**6),
-    )(*[in_hbm(x.T) for x in (pick_mask, arrival, quality)])
+    )(*[in_hbm(x) for x in (pick_mask.T, arrival.T, quality.T, cell_index, station_xyz)])
     picks = lax.all_to_all(packed, "cell", 0, 0, axis_index_groups=[rotated(n_cell, first_picks)])
     travel = call(
         travel_kernel,
-        [vmem] * 6 + [hbm, vmem],
+        [vmem] * 8,
         shape((stations, cells), f32),
         "travel",
-        [
-            pltpu.VMEM((stations * cells, w_cell.shape[1]), jnp.bfloat16),
-            pltpu.VMEM(bias_hidden.shape, f32),
-            pltpu.SemaphoreType.DMA,
-        ],
+        [pltpu.VMEM((stations * cells, w_cell.shape[1]), jnp.bfloat16)],
     )(
         cell_index,
         station_xyz,
@@ -205,14 +219,11 @@
         w_station,
         bias_in[None],
         w_hidden,
-        in_hbm(bias_hidden),
+        bias_hidden,
         w_out[None],
     )
-    blocks = call(join_kernel, [vmem] * 2, shape((n_cell, 3, stations, cells), f32), "join")(travel, picks)
-    equal_cores = [[2 * chip + core for chip in rotated(n_cell, first_blocks)] for core in range(2)]
-    pairs = [[2 * chip + core for core in pair_order] for chip in range(n_cell)]
-    blocks = lax.all_to_all(blocks, "sta", 0, 0, axis_index_groups=equal_cores)
-    blocks = lax.all_gather(blocks, "sta", axis_index_groups=pairs)
+    blocks = call(join_kernel, [vmem] * 2, shape((n_sta, 2, stations, cells), f32), "join")(travel, picks)
+    blocks = lax.all_to_all(blocks, "sta", 0, 0, axis_index_groups=[rotated(n_sta, first_blocks)])
     logit, stats = call(
         logit_kernel,
         [vmem],

time: 51.7 us -> 51.7 us (level)
  waiting for transfers between devices: 2.74 us -> 3.35 us
  Pallas kernels: 5.68 us -> 5.12 us
    all_to_all x1, blocking collectives: 13.5 us -> 15.7 us  [per_device(): lax.all_to_all(blocks, 'sta', 0, 0, axis_index_groups=[rotated(n_sta, fir...]
    all_gather x1 -> x0, blocking collectives: 2.08 us -> none  [per_device(): blocks = lax.all_gather(blocks, 'sta', axis_index_groups=pairs)]
    all_to_all x1, waiting for transfers between devices: 2.74 us -> 3.35 us  [per_device(): lax.all_to_all(packed, 'cell', 0, 0, axis_index_groups=[rotated(n_cell, f...]
  transfers between devices with their start and end apart: 1 -> 1, of which waited for: 1 -> 1; matrix products, arithmetic and copies ran while one was open for 0% -> 0% of each run, Pallas kernels for 5% -> 4%
where the time goes in v7:
time: 51.7 us; the launch traced here: 51.3 us
  blocking collectives  27.5 us (53%)
  starting transfers between devices  14.6 us (28%)
  Pallas kernels  5.12 us (10%)
  waiting for transfers between devices  3.35 us (6%)
  local copies, waits for them, and re-layouts  0.67 us (1%)
    all_to_all x1, blocking collectives, per_device(): lax.all_to_all(blocks, 'sta', 0, 0, axis_index_groups=[rotated(n_sta, fir...  15.7 us
    all_to_all x1, starting transfers between devices, per_device(): lax.all_to_all(packed, 'cell', 0, 0, axis_index_groups=[rotated(n_cell, f...  14.6 us
    all_to_all x1, blocking collectives, per_device(): lax.all_to_all(stats, 'cell', 0, 0, axis_index_groups=[rotated(n_cell, fi...  11.8 us
    all_to_all x1, waiting for transfers between devices, per_device(): lax.all_to_all(packed, 'cell', 0, 0, axis_index_groups=[rotated(n_cell, f...  3.35 us
    pallas_call x1, Pallas kernels, per_device(): call(travel_kernel, [vmem] * 8, shape((stations, cells), f32), 'travel',...  2.05 us
    pallas_call x1, Pallas kernels, per_device(): call(pack_kernel, [hbm] * 5, (shape((n_cell, 2, stations, events), f32),...  1.53 us
  transfers between devices with their start and end apart: 1, of which 1 were waited for; matrix products, arithmetic and copies ran while one was open for 0% of the time, Pallas kernels for 4%

profile of v7, /device:TPU:6, one launch (start us, length us, event | category | flops | bytes accessed | tf_op | source)
XLA Modules:
  0.0 51.3 jit_solution(881380035741863724)
XLA Ops:
  0.0 0.0 copy-start
  0.0 1.5 %pack.1 = (f32[16,2,8,128]{3,2,1,0:T(8,128)}, s32[3,128]{1,0:T(4,128)S(1)}, f32[3,8]{1,0:T(4,128)S(1)}) custom-call(s32[8,128]{1,0:T(8,128)} %bitcast.5, f32[8,128]{1,0:T(8,128)} %bitcast.6, f32[8,128]{1,0:T(8,128)} %bitcast.7, s32[3,128]{1,0:T(4,128)} %cell_hbm.1, f32[3,8]{1,0:T(4,128)} %station_hbm.1), custom_call_target="tpu_custom_call" | custom-call | flops 2000000000 | bytes 1000000 | tf_op jit(solution)/shard_map/pack/pallas_call | solution.py:191
  1.5 0.0 copy-start.5
  1.6 0.0 copy-start.2
  1.6 0.0 copy-start.3
  1.6 0.0 copy-start.4
  1.6 14.6 %all-to-all-start = ((f32[16,2,8,128]{3,2,1,0:T(8,128)}), f32[16,2,8,128]{3,2,1,0:T(8,128)S(1)}, u32[]{:S(2)}, u32[]{:S(2)}) async-start(f32[16,2,8,128]{3,2,1,0:T(8,128)} %get-tuple-element.12), calls=%async_computation | async-start | bytes 262144 | tf_op jit(solution)/shard_map/all_to_all | solution.py:208
  16.2 0.0 copy-done.5
  16.2 0.0 copy-start.1
  16.2 0.0 copy-done
  16.2 0.0 copy-done.2
  16.2 0.0 copy-done.3
  16.2 0.0 copy-done.4
  16.2 0.6 %copy-done.1 = f32[3,512]{1,0:T(4,128)S(1)} copy-done((f32[3,512]{1,0:T(4,128)S(1)}, f32[3,512]{1,0:T(4,128)}, u32[]{:S(2)}) %copy-start.1) | copy-done | bytes 6168
  16.9 2.0 %travel.1.travel_ref = f32[8,128]{1,0:T(8,128)S(1)} custom-call(s32[3,128]{1,0:T(4,128)S(1)} %get-tuple-element.10.cell_ref, f32[3,8]{1,0:T(4,128)S(1)} %get-tuple-element.11.station_ref, f32[3,512]{1,0:T(4,128)S(1)} %copy-done.1, f32[3,512]{1,0:T(4,128)S(1)} %copy-done.2, f32[1,512]{1,0:T(1,128)S(1)} %bitcast.4, bf16[2,512,512]{2,1,0:T(8,128)(2,1)S(1)} %copy-done, ...), custom_call_target="tpu_custom_call" | custom-call | tf_op jit(solution)/shard_map/travel/pallas_call | solution.py:209
  18.9 3.3 %all-to-all-done.picks_ref = f32[16,2,8,128]{3,2,1,0:T(8,128)S(1)} async-done(((f32[16,2,8,128]{3,2,1,0:T(8,128)}), f32[16,2,8,128]{3,2,1,0:T(8,128)S(1)}, u32[]{:S(2)}, u32[]{:S(2)}) %all-to-all-start) | async-done | bytes 131104 | tf_op jit(solution)/shard_map/all_to_all | solution.py:208
  22.3 0.1 join.1
  22.4 15.7 %all_to_all.15.blocks_ref = f32[32,2,8,128]{3,2,1,0:T(8,128)S(1)} all-to-all(f32[32,2,8,128]{3,2,1,0:T(8,128)S(1)} %join.1), channel_id=1, replica_groups={{25,26,27,28,29,30,31,0,1,2,3,4,5,6,7,8,9,10,11,12,13,14,15,16,17,18,19..., dimensions={0} | all-to-all | bytes 524288 | tf_op jit(solution)/shard_map/all_to_all | solution.py:226
  38.1 0.6 %logit.1 = (f32[64,128]{1,0:T(8,128)S(1)}, f32[16,1,128]{2,1,0:T(1,128)S(1)}) custom-call(f32[32,2,8,128]{3,2,1,0:T(8,128)S(1)} %all_to_all.15.blocks_ref), custom_call_target="tpu_custom_call" | custom-call | tf_op jit(solution)/shard_map/logit/pallas_call | solution.py:227
  38.7 11.8 %all_to_all.16.stats_ref = f32[16,1,128]{2,1,0:T(1,128)S(1)} all-to-all(f32[16,1,128]{2,1,0:T(1,128)S(1)} %get-tuple-element.14), channel_id=1, replica_groups={{384,416,448,480,0,32,64,96,128,160,192,224,256,288,320,352},{385,417,4..., dimensions={0} | all-to-all | bytes 16384 | tf_op jit(solution)/shard_map/all_to_all | solution.py:233
  50.5 0.9 %final.1 = f32[64,128]{1,0:T(8,128)} custom-call(f32[64,128]{1,0:T(8,128)S(1)} %get-tuple-element.13.logit_ref, f32[16,1,128]{2,1,0:T(1,128)S(1)} %all_to_all.16.stats_ref), custom_call_target="tpu_custom_call" | custom-call | tf_op jit(solution)/shard_map/final/pallas_call | solution.py:234
  (1 shorter events, 0.0 us)
Async XLA Ops:
  0.0 16.2 %copy-start = (bf16[2,512,512]{2,1,0:T(8,128)(2,1)S(1)}, bf16[2,512,512]{2,1,0:T(8,128)(2,1)}, u32[]{:S(2)}) copy-start(bf16[2,512,512]{2,1,0:T(8,128)(2,1)} %w_hidden_ref.1) | copy-start | bytes 3145732
  1.5 14.6 %copy-start.5 = (bf16[512]{0:T(512)(128)(2,1)S(1)}, bf16[512]{0:T(512)(128)(2,1)}, u32[]{:S(2)}) copy-start(bf16[512]{0:T(512)(128)(2,1)} %param.18) | copy-start | bytes 3076
  1.6 14.7 %copy-start.2 = (f32[3,512]{1,0:T(4,128)S(1)}, f32[3,512]{1,0:T(4,128)}, u32[]{:S(2)}) copy-start(f32[3,512]{1,0:T(4,128)} %w_station_ref.1) | copy-start | bytes 18436
  1.6 14.7 %copy-start.3 = (f32[2,512]{1,0:T(2,128)S(1)}, f32[2,512]{1,0:T(2,128)}, u32[]{:S(2)}) copy-start(f32[2,512]{1,0:T(2,128)} %bias_hidden_ref.1) | copy-start | bytes 12292
  1.6 14.7 %copy-start.4 = (f32[512]{0:T(512)S(1)}, f32[512]{0:T(512)}, u32[]{:S(2)}) copy-start(f32[512]{0:T(512)} %param.15) | copy-start | bytes 6148
  1.6 20.7 %all-to-all-start = ((f32[16,2,8,128]{3,2,1,0:T(8,128)}), f32[16,2,8,128]{3,2,1,0:T(8,128)S(1)}, u32[]{:S(2)}, u32[]{:S(2)}) async-start(f32[16,2,8,128]{3,2,1,0:T(8,128)} %get-tuple-element.12), calls=%async_computation | async-start | bytes 262144 | tf_op jit(solution)/shard_map/all_to_all | solution.py:208
  16.2 0.7 %copy-start.1 = (f32[3,512]{1,0:T(4,128)S(1)}, f32[3,512]{1,0:T(4,128)}, u32[]{:S(2)}) copy-start(f32[3,512]{1,0:T(4,128)} %w_cell_ref.1) | copy-start | bytes 18436

commit v8 on v7

--- a/solution.py
+++ b/solution.py
@@ -6,7 +6,8 @@
 from jax.sharding import PartitionSpec as P
 
 grid_step = 0.015625
-first_picks, first_blocks, first_stats = 12, 25, 12
+first_picks, first_blocks, first_stats = 12, 13, 12
+pair_order = (0, 1)
 highest = lax.Precision.HIGHEST
 
 
@@ -98,24 +99,22 @@
 def join_kernel(travel_ref, picks_ref, out_ref):
     travel = travel_ref[...]
     peers = out_ref.shape[0]
-    for place, member in enumerate(rotated(peers, first_blocks)):
-        chip, core = divmod(member, 2)
+    for place, chip in enumerate(rotated(peers, first_blocks)):
         out_ref[place, 0] = travel
-        w = picks_ref[rotated(peers // 2, first_picks).index(chip), 0]
-        a = picks_ref[rotated(peers // 2, first_picks).index(chip), 1]
-        half = w.shape[1] // 2
-        part = slice(core * half, (core + 1) * half)
-        out_ref[place, 1] = jnp.concatenate([w[:, part], a[:, part]], axis=1)
+        for k in range(2):
+            out_ref[place, 1 + k] = picks_ref[rotated(peers, first_picks).index(chip), k]
 
 
 def logit_kernel(blocks_ref, logit_ref, stats_ref):
-    peers, _, rows, width = blocks_ref.shape
+    cores, peers, _, rows, width = blocks_ref.shape
     half = width // 2
-    travel, picks = [
-        blocks_ref[:, k].reshape(peers * rows, width) for k in range(2)
+    odd = lax.axis_index("sta") % 2 == 1
+    travel, weight, arrival = [
+        blocks_ref[:, :, k].reshape(cores * peers * rows, width) for k in range(3)
     ]
-    picks = picks.T
-    weight, arrival = picks[:half], picks[half:]
+    weight, arrival = [
+        jnp.where(odd, member[half:], member[:half]) for member in (weight.T, arrival.T)
+    ]
     weighted = weight * arrival
     sq_sum = jnp.sum(weighted * arrival, axis=1, keepdims=True)
     mean_sum = jnp.sum(weighted, axis=1, keepdims=True)
@@ -222,8 +221,11 @@
         bias_hidden,
         w_out[None],
     )
-    blocks = call(join_kernel, [vmem] * 2, shape((n_sta, 2, stations, cells), f32), "join")(travel, picks)
-    blocks = lax.all_to_all(blocks, "sta", 0, 0, axis_index_groups=[rotated(n_sta, first_blocks)])
+    blocks = call(join_kernel, [vmem] * 2, shape((n_cell, 3, stations, cells), f32), "join")(travel, picks)
+    equal_cores = [[2 * chip + core for chip in rotated(n_cell, first_blocks)] for core in range(2)]
+    pairs = [[2 * chip + core for core in pair_order] for chip in range(n_cell)]
+    blocks = lax.all_to_all(blocks, "sta", 0, 0, axis_index_groups=equal_cores)
+    blocks = lax.all_gather(blocks, "sta", axis_index_groups=pairs)
     logit, stats = call(
         logit_kernel,
         [vmem],

time: 51.7 us -> 51.4 us (level)
    all_to_all x1, blocking collectives: 15.7 us -> 13.2 us  [per_device(): blocks = lax.all_to_all(blocks, 'sta', 0, 0, axis_index_groups=equal_cores)]
    all_gather x0 -> x1, blocking collectives: none -> 2.08 us  [per_device(): blocks = lax.all_gather(blocks, 'sta', axis_index_groups=pairs)]
where the time goes in v8:
time: 51.4 us; the launch traced here: 50.9 us
  blocking collectives  27.1 us (53%)
  starting transfers between devices  14.6 us (28%)
  Pallas kernels  5.09 us (10%)
  waiting for transfers between devices  3.35 us (7%)
  local copies, waits for them, and re-layouts  0.67 us (1%)
    all_to_all x1, starting transfers between devices, per_device(): lax.all_to_all(packed, 'cell', 0, 0, axis_index_groups=[rotated(n_cell, f...  14.6 us
    all_to_all x1, blocking collectives, per_device(): blocks = lax.all_to_all(blocks, 'sta', 0, 0, axis_index_groups=equal_cores)  13.2 us
    all_to_all x1, blocking collectives, per_device(): lax.all_to_all(stats, 'cell', 0, 0, axis_index_groups=[rotated(n_cell, fi...  11.9 us
    all_to_all x1, waiting for transfers between devices, per_device(): lax.all_to_all(packed, 'cell', 0, 0, axis_index_groups=[rotated(n_cell, f...  3.35 us
    all_gather x1, blocking collectives, per_device(): blocks = lax.all_gather(blocks, 'sta', axis_index_groups=pairs)  2.08 us
    pallas_call x1, Pallas kernels, per_device(): call(travel_kernel, [vmem] * 8, shape((stations, cells), f32), 'travel',...  2.05 us
    pallas_call x1, Pallas kernels, per_device(): call(pack_kernel, [hbm] * 5, (shape((n_cell, 2, stations, events), f32),...  1.53 us
  transfers between devices with their start and end apart: 1, of which 1 were waited for; matrix products, arithmetic and copies ran while one was open for 0% of the time, Pallas kernels for 4%

profile of v8, /device:TPU:6, one launch (start us, length us, event | category | flops | bytes accessed | tf_op | source)
XLA Modules:
  0.0 50.9 jit_solution(1009529179334454095)
XLA Ops:
  0.0 0.0 copy-start
  0.0 1.5 %pack.1 = (f32[16,2,8,128]{3,2,1,0:T(8,128)}, s32[3,128]{1,0:T(4,128)S(1)}, f32[3,8]{1,0:T(4,128)S(1)}) custom-call(s32[8,128]{1,0:T(8,128)} %bitcast.7, f32[8,128]{1,0:T(8,128)} %bitcast.8, f32[8,128]{1,0:T(8,128)} %bitcast.9, s32[3,128]{1,0:T(4,128)} %cell_hbm.1, f32[3,8]{1,0:T(4,128)} %station_hbm.1), custom_call_target="tpu_custom_call" | custom-call | flops 2000000000 | bytes 1000000 | tf_op jit(solution)/shard_map/pack/pallas_call | solution.py:190
  1.5 0.0 copy-start.5
  1.6 0.0 copy-start.2
  1.6 0.0 copy-start.3
  1.6 0.0 copy-start.4
  1.6 14.6 %all-to-all-start = ((f32[16,2,8,128]{3,2,1,0:T(8,128)}), f32[16,2,8,128]{3,2,1,0:T(8,128)S(1)}, u32[]{:S(2)}, u32[]{:S(2)}) async-start(f32[16,2,8,128]{3,2,1,0:T(8,128)} %get-tuple-element.12), calls=%async_computation | async-start | bytes 262144 | tf_op jit(solution)/shard_map/all_to_all | solution.py:207
  16.2 0.0 copy-done.5
  16.2 0.0 copy-start.1
  16.2 0.0 copy-done
  16.2 0.0 copy-done.2
  16.2 0.0 copy-done.3
  16.2 0.0 copy-done.4
  16.2 0.6 %copy-done.1 = f32[3,512]{1,0:T(4,128)S(1)} copy-done((f32[3,512]{1,0:T(4,128)S(1)}, f32[3,512]{1,0:T(4,128)}, u32[]{:S(2)}) %copy-start.1) | copy-done | bytes 6168
  16.9 2.0 %travel.1.travel_ref = f32[8,128]{1,0:T(8,128)S(1)} custom-call(s32[3,128]{1,0:T(4,128)S(1)} %get-tuple-element.10.cell_ref, f32[3,8]{1,0:T(4,128)S(1)} %get-tuple-element.11.station_ref, f32[3,512]{1,0:T(4,128)S(1)} %copy-done.1, f32[3,512]{1,0:T(4,128)S(1)} %copy-done.2, f32[1,512]{1,0:T(1,128)S(1)} %bitcast.6, bf16[2,512,512]{2,1,0:T(8,128)(2,1)S(1)} %copy-done, ...), custom_call_target="tpu_custom_call" | custom-call | tf_op jit(solution)/shard_map/travel/pallas_call | solution.py:208
  18.9 3.3 %all-to-all-done.picks_ref = f32[16,2,8,128]{3,2,1,0:T(8,128)S(1)} async-done(((f32[16,2,8,128]{3,2,1,0:T(8,128)}), f32[16,2,8,128]{3,2,1,0:T(8,128)S(1)}, u32[]{:S(2)}, u32[]{:S(2)}) %all-to-all-start) | async-done | bytes 131104 | tf_op jit(solution)/shard_map/all_to_all | solution.py:207
  22.3 13.2 %all_to_all.15 = f32[16,3,8,128]{3,2,1,0:T(8,128)S(1)} all-to-all(f32[16,3,8,128]{3,2,1,0:T(8,128)S(1)} %join.1), channel_id=1, replica_groups={{26,28,30,0,2,4,6,8,10,12,14,16,18,20,22,24},{27,29,31,1,3,5,7,9,11,13,..., dimensions={0} | all-to-all | bytes 393216 | tf_op jit(solution)/shard_map/all_to_all | solution.py:227
  35.5 2.1 %all-gather = f32[32,3,8,128]{3,2,1,0:T(8,128)S(1)} all-gather(f32[16,3,8,128]{3,2,1,0:T(8,128)S(1)} %all_to_all.15), channel_id=2, replica_groups={{0,1},{2,3},{4,5},{6,7},{8,9},{10,11},{12,13},{14,15},{16,17},{18,19},{..., dimensions={0}, use_global_device_ids=true | all-gather | bytes 589824 | tf_op jit(solution)/shard_map/all_gather | solution.py:228
  37.5 0.6 %logit.1 = (f32[64,128]{1,0:T(8,128)S(1)}, f32[16,1,128]{2,1,0:T(1,128)S(1)}) custom-call(f32[2,16,3,8,128]{4,3,2,1,0:T(8,128)S(1)} %bitcast.5), custom_call_target="tpu_custom_call" | custom-call | tf_op jit(solution)/shard_map/logit/pallas_call | solution.py:229
  38.2 11.9 %all_to_all.16.stats_ref = f32[16,1,128]{2,1,0:T(1,128)S(1)} all-to-all(f32[16,1,128]{2,1,0:T(1,128)S(1)} %get-tuple-element.14), channel_id=1, replica_groups={{384,416,448,480,0,32,64,96,128,160,192,224,256,288,320,352},{385,417,4..., dimensions={0} | all-to-all | bytes 16384 | tf_op jit(solution)/shard_map/all_to_all | solution.py:235
  50.1 0.9 %final.1 = f32[64,128]{1,0:T(8,128)} custom-call(f32[64,128]{1,0:T(8,128)S(1)} %get-tuple-element.13.logit_ref, f32[16,1,128]{2,1,0:T(1,128)S(1)} %all_to_all.16.stats_ref), custom_call_target="tpu_custom_call" | custom-call | tf_op jit(solution)/shard_map/final/pallas_call | solution.py:236
  (2 shorter events, 0.0 us)
Async XLA Ops:
  0.0 16.2 %copy-start = (bf16[2,512,512]{2,1,0:T(8,128)(2,1)S(1)}, bf16[2,512,512]{2,1,0:T(8,128)(2,1)}, u32[]{:S(2)}) copy-start(bf16[2,512,512]{2,1,0:T(8,128)(2,1)} %w_hidden_ref.1) | copy-start | bytes 3145732
  1.5 14.6 %copy-start.5 = (bf16[512]{0:T(512)(128)(2,1)S(1)}, bf16[512]{0:T(512)(128)(2,1)}, u32[]{:S(2)}) copy-start(bf16[512]{0:T(512)(128)(2,1)} %param.18) | copy-start | bytes 3076
  1.6 14.7 %copy-start.2 = (f32[3,512]{1,0:T(4,128)S(1)}, f32[3,512]{1,0:T(4,128)}, u32[]{:S(2)}) copy-start(f32[3,512]{1,0:T(4,128)} %w_station_ref.1) | copy-start | bytes 18436
  1.6 14.7 %copy-start.3 = (f32[2,512]{1,0:T(2,128)S(1)}, f32[2,512]{1,0:T(2,128)}, u32[]{:S(2)}) copy-start(f32[2,512]{1,0:T(2,128)} %bias_hidden_ref.1) | copy-start | bytes 12292
  1.6 14.7 %copy-start.4 = (f32[512]{0:T(512)S(1)}, f32[512]{0:T(512)}, u32[]{:S(2)}) copy-start(f32[512]{0:T(512)} %param.15) | copy-start | bytes 6148
  1.6 20.7 %all-to-all-start = ((f32[16,2,8,128]{3,2,1,0:T(8,128)}), f32[16,2,8,128]{3,2,1,0:T(8,128)S(1)}, u32[]{:S(2)}, u32[]{:S(2)}) async-start(f32[16,2,8,128]{3,2,1,0:T(8,128)} %get-tuple-element.12), calls=%async_computation | async-start | bytes 262144 | tf_op jit(solution)/shard_map/all_to_all | solution.py:207
  16.2 0.7 %copy-start.1 = (f32[3,512]{1,0:T(4,128)S(1)}, f32[3,512]{1,0:T(4,128)}, u32[]{:S(2)}) copy-start(f32[3,512]{1,0:T(4,128)} %w_cell_ref.1) | copy-start | bytes 18436

commit v9 on v8

--- a/solution.py
+++ b/solution.py
@@ -6,7 +6,7 @@
 from jax.sharding import PartitionSpec as P
 
 grid_step = 0.015625
-first_picks, first_blocks, first_stats = 12, 13, 12
+first_picks, first_blocks, first_stats = 13, 13, 12
 pair_order = (0, 1)
 highest = lax.Precision.HIGHEST
 

time: 51.4 us -> 51.2 us (level)
  starting transfers between devices: 14.6 us -> 13.7 us
  waiting for transfers between devices: 3.35 us -> 3.9 us
    all_to_all x1, starting transfers between devices: 14.6 us -> 13.7 us  [per_device(): lax.all_to_all(packed, 'cell', 0, 0, axis_index_groups=[rotated(n_cell, f...]
    all_to_all x1, waiting for transfers between devices: 3.35 us -> 3.9 us  [per_device(): lax.all_to_all(packed, 'cell', 0, 0, axis_index_groups=[rotated(n_cell, f...]
where the time goes in v9:
time: 51.2 us; the launch traced here: 50.8 us
  blocking collectives  27.4 us (54%)
  starting transfers between devices  13.7 us (27%)
  Pallas kernels  5.1 us (10%)
  waiting for transfers between devices  3.9 us (8%)
  local copies, waits for them, and re-layouts  0.67 us (1%)
    all_to_all x1, starting transfers between devices, per_device(): lax.all_to_all(packed, 'cell', 0, 0, axis_index_groups=[rotated(n_cell, f...  13.7 us
    all_to_all x1, blocking collectives, per_device(): blocks = lax.all_to_all(blocks, 'sta', 0, 0, axis_index_groups=equal_cores)  13.2 us
    all_to_all x1, blocking collectives, per_device(): lax.all_to_all(stats, 'cell', 0, 0, axis_index_groups=[rotated(n_cell, fi...  12.1 us
    all_to_all x1, waiting for transfers between devices, per_device(): lax.all_to_all(packed, 'cell', 0, 0, axis_index_groups=[rotated(n_cell, f...  3.9 us
    all_gather x1, blocking collectives, per_device(): blocks = lax.all_gather(blocks, 'sta', axis_index_groups=pairs)  2.08 us
    pallas_call x1, Pallas kernels, per_device(): call(travel_kernel, [vmem] * 8, shape((stations, cells), f32), 'travel',...  2.05 us
    pallas_call x1, Pallas kernels, per_device(): call(pack_kernel, [hbm] * 5, (shape((n_cell, 2, stations, events), f32),...  1.53 us
  transfers between devices with their start and end apart: 1, of which 1 were waited for; matrix products, arithmetic and copies ran while one was open for 0% of the time, Pallas kernels for 4%

profile of v9, /device:TPU:6, one launch (start us, length us, event | category | flops | bytes accessed | tf_op | source)
XLA Modules:
  0.0 50.8 jit_solution(13702216782466220499)
XLA Ops:
  0.0 0.0 copy-start
  0.0 1.5 %pack.1 = (f32[16,2,8,128]{3,2,1,0:T(8,128)}, s32[3,128]{1,0:T(4,128)S(1)}, f32[3,8]{1,0:T(4,128)S(1)}) custom-call(s32[8,128]{1,0:T(8,128)} %bitcast.7, f32[8,128]{1,0:T(8,128)} %bitcast.8, f32[8,128]{1,0:T(8,128)} %bitcast.9, s32[3,128]{1,0:T(4,128)} %cell_hbm.1, f32[3,8]{1,0:T(4,128)} %station_hbm.1), custom_call_target="tpu_custom_call" | custom-call | flops 2000000000 | bytes 1000000 | tf_op jit(solution)/shard_map/pack/pallas_call | solution.py:190
  1.5 0.0 copy-start.5
  1.6 0.0 copy-start.2
  1.6 0.0 copy-start.3
  1.6 0.0 copy-start.4
  1.6 13.7 %all-to-all-start = ((f32[16,2,8,128]{3,2,1,0:T(8,128)}), f32[16,2,8,128]{3,2,1,0:T(8,128)S(1)}, u32[]{:S(2)}, u32[]{:S(2)}) async-start(f32[16,2,8,128]{3,2,1,0:T(8,128)} %get-tuple-element.12), calls=%async_computation | async-start | bytes 262144 | tf_op jit(solution)/shard_map/all_to_all | solution.py:207
  15.3 0.0 copy-done.5
  15.3 0.0 copy-start.1
  15.3 0.0 copy-done
  15.3 0.0 copy-done.2
  15.3 0.0 copy-done.3
  15.3 0.0 copy-done.4
  15.3 0.6 %copy-done.1 = f32[3,512]{1,0:T(4,128)S(1)} copy-done((f32[3,512]{1,0:T(4,128)S(1)}, f32[3,512]{1,0:T(4,128)}, u32[]{:S(2)}) %copy-start.1) | copy-done | bytes 6168
  16.0 2.1 %travel.1.travel_ref = f32[8,128]{1,0:T(8,128)S(1)} custom-call(s32[3,128]{1,0:T(4,128)S(1)} %get-tuple-element.10.cell_ref, f32[3,8]{1,0:T(4,128)S(1)} %get-tuple-element.11.station_ref, f32[3,512]{1,0:T(4,128)S(1)} %copy-done.1, f32[3,512]{1,0:T(4,128)S(1)} %copy-done.2, f32[1,512]{1,0:T(1,128)S(1)} %bitcast.6, bf16[2,512,512]{2,1,0:T(8,128)(2,1)S(1)} %copy-done, ...), custom_call_target="tpu_custom_call" | custom-call | tf_op jit(solution)/shard_map/travel/pallas_call | solution.py:208
  18.0 3.9 %all-to-all-done.picks_ref = f32[16,2,8,128]{3,2,1,0:T(8,128)S(1)} async-done(((f32[16,2,8,128]{3,2,1,0:T(8,128)}), f32[16,2,8,128]{3,2,1,0:T(8,128)S(1)}, u32[]{:S(2)}, u32[]{:S(2)}) %all-to-all-start) | async-done | bytes 131104 | tf_op jit(solution)/shard_map/all_to_all | solution.py:207
  21.9 13.2 %all_to_all.15 = f32[16,3,8,128]{3,2,1,0:T(8,128)S(1)} all-to-all(f32[16,3,8,128]{3,2,1,0:T(8,128)S(1)} %join.1), channel_id=1, replica_groups={{26,28,30,0,2,4,6,8,10,12,14,16,18,20,22,24},{27,29,31,1,3,5,7,9,11,13,..., dimensions={0} | all-to-all | bytes 393216 | tf_op jit(solution)/shard_map/all_to_all | solution.py:227
  35.1 2.1 %all-gather = f32[32,3,8,128]{3,2,1,0:T(8,128)S(1)} all-gather(f32[16,3,8,128]{3,2,1,0:T(8,128)S(1)} %all_to_all.15), channel_id=2, replica_groups={{0,1},{2,3},{4,5},{6,7},{8,9},{10,11},{12,13},{14,15},{16,17},{18,19},{..., dimensions={0}, use_global_device_ids=true | all-gather | bytes 589824 | tf_op jit(solution)/shard_map/all_gather | solution.py:228
  37.2 0.6 %logit.1 = (f32[64,128]{1,0:T(8,128)S(1)}, f32[16,1,128]{2,1,0:T(1,128)S(1)}) custom-call(f32[2,16,3,8,128]{4,3,2,1,0:T(8,128)S(1)} %bitcast.5), custom_call_target="tpu_custom_call" | custom-call | tf_op jit(solution)/shard_map/logit/pallas_call | solution.py:229
  37.8 12.1 %all_to_all.16.stats_ref = f32[16,1,128]{2,1,0:T(1,128)S(1)} all-to-all(f32[16,1,128]{2,1,0:T(1,128)S(1)} %get-tuple-element.14), channel_id=1, replica_groups={{384,416,448,480,0,32,64,96,128,160,192,224,256,288,320,352},{385,417,4..., dimensions={0} | all-to-all | bytes 16384 | tf_op jit(solution)/shard_map/all_to_all | solution.py:235
  50.0 0.9 %final.1 = f32[64,128]{1,0:T(8,128)} custom-call(f32[64,128]{1,0:T(8,128)S(1)} %get-tuple-element.13.logit_ref, f32[16,1,128]{2,1,0:T(1,128)S(1)} %all_to_all.16.stats_ref), custom_call_target="tpu_custom_call" | custom-call | tf_op jit(solution)/shard_map/final/pallas_call | solution.py:236
  (2 shorter events, 0.0 us)
Async XLA Ops:
  0.0 15.3 %copy-start = (bf16[2,512,512]{2,1,0:T(8,128)(2,1)S(1)}, bf16[2,512,512]{2,1,0:T(8,128)(2,1)}, u32[]{:S(2)}) copy-start(bf16[2,512,512]{2,1,0:T(8,128)(2,1)} %w_hidden_ref.1) | copy-start | bytes 3145732
  1.5 13.7 %copy-start.5 = (bf16[512]{0:T(512)(128)(2,1)S(1)}, bf16[512]{0:T(512)(128)(2,1)}, u32[]{:S(2)}) copy-start(bf16[512]{0:T(512)(128)(2,1)} %param.18) | copy-start | bytes 3076
  1.6 13.8 %copy-start.2 = (f32[3,512]{1,0:T(4,128)S(1)}, f32[3,512]{1,0:T(4,128)}, u32[]{:S(2)}) copy-start(f32[3,512]{1,0:T(4,128)} %w_station_ref.1) | copy-start | bytes 18436
  1.6 13.8 %copy-start.3 = (f32[2,512]{1,0:T(2,128)S(1)}, f32[2,512]{1,0:T(2,128)}, u32[]{:S(2)}) copy-start(f32[2,512]{1,0:T(2,128)} %bias_hidden_ref.1) | copy-start | bytes 12292
  1.6 13.8 %copy-start.4 = (f32[512]{0:T(512)S(1)}, f32[512]{0:T(512)}, u32[]{:S(2)}) copy-start(f32[512]{0:T(512)} %param.15) | copy-start | bytes 6148
  1.6 20.3 %all-to-all-start = ((f32[16,2,8,128]{3,2,1,0:T(8,128)}), f32[16,2,8,128]{3,2,1,0:T(8,128)S(1)}, u32[]{:S(2)}, u32[]{:S(2)}) async-start(f32[16,2,8,128]{3,2,1,0:T(8,128)} %get-tuple-element.12), calls=%async_computation | async-start | bytes 262144 | tf_op jit(solution)/shard_map/all_to_all | solution.py:207
  15.3 0.7 %copy-start.1 = (f32[3,512]{1,0:T(4,128)S(1)}, f32[3,512]{1,0:T(4,128)}, u32[]{:S(2)}) copy-start(f32[3,512]{1,0:T(4,128)} %w_cell_ref.1) | copy-start | bytes 18436

commit v10 on v9

--- a/solution.py
+++ b/solution.py
@@ -21,9 +21,11 @@
     quality_hbm,
     cell_hbm,
     station_hbm,
+    w_cell_hbm,
     out_ref,
     cell_ref,
     station_ref,
+    w_cell_ref,
     mask_ref,
     arrival_ref,
     quality_ref,
@@ -35,6 +37,7 @@
         (quality_hbm, quality_ref),
         (cell_hbm, cell_ref),
         (station_hbm, station_ref),
+        (w_cell_hbm, w_cell_ref),
     )
     copies = [pltpu.make_async_copy(*pair, sems.at[k]) for k, pair in enumerate(pairs)]
     for copy in copies:
@@ -187,23 +190,24 @@
     cells = cell_index.shape[1]
     f32 = jnp.float32
     shape = jax.ShapeDtypeStruct
-    packed, cell_index, station_xyz = call(
+    packed, cell_index, station_xyz, w_cell = call(
         pack_kernel,
-        [hbm] * 5,
+        [hbm] * 6,
         (
             shape((n_cell, 2, stations, events), f32),
             shape(cell_index.shape, cell_index.dtype),
             shape(station_xyz.shape, f32),
+            shape(w_cell.shape, f32),
         ),
         "pack",
         [
             pltpu.VMEM((stations, events), pick_mask.dtype),
             pltpu.VMEM((stations, events), f32),
             pltpu.VMEM((stations, events), f32),
-            pltpu.SemaphoreType.DMA((5,)),
+            pltpu.SemaphoreType.DMA((6,)),
         ],
         pl.CostEstimate(flops=2 * 10**9, transcendentals=0, bytes_accessed=10**6),
-    )(*[in_hbm(x) for x in (pick_mask.T, arrival.T, quality.T, cell_index, station_xyz)])
+    )(*[in_hbm(x) for x in (pick_mask.T, arrival.T, quality.T, cell_index, station_xyz, w_cell)])
     picks = lax.all_to_all(packed, "cell", 0, 0, axis_index_groups=[rotated(n_cell, first_picks)])
     travel = call(
         travel_kernel,

time: 51.2 us -> 51.2 us (level)
  no operation moved by 1% of the time
where the time goes in v10:
time: 51.2 us; the launch traced here: 50.7 us
  blocking collectives  27.4 us (54%)
  starting transfers between devices  13.5 us (26%)
  Pallas kernels  5.14 us (10%)
  waiting for transfers between devices  3.89 us (8%)
  local copies, waits for them, and re-layouts  0.68 us (1%)
    all_to_all x1, starting transfers between devices, per_device(): lax.all_to_all(packed, 'cell', 0, 0, axis_index_groups=[rotated(n_cell, f...  13.5 us
    all_to_all x1, blocking collectives, per_device(): blocks = lax.all_to_all(blocks, 'sta', 0, 0, axis_index_groups=equal_cores)  13.2 us
    all_to_all x1, blocking collectives, per_device(): lax.all_to_all(stats, 'cell', 0, 0, axis_index_groups=[rotated(n_cell, fi...  12.2 us
    all_to_all x1, waiting for transfers between devices, per_device(): lax.all_to_all(packed, 'cell', 0, 0, axis_index_groups=[rotated(n_cell, f...  3.89 us
    all_gather x1, blocking collectives, per_device(): blocks = lax.all_gather(blocks, 'sta', axis_index_groups=pairs)  2.08 us
    pallas_call x1, Pallas kernels, per_device(): call(travel_kernel, [vmem] * 8, shape((stations, cells), f32), 'travel',...  2.05 us
    pallas_call x1, Pallas kernels, per_device(): call(pack_kernel, [hbm] * 6, (shape((n_cell, 2, stations, events), f32),...  1.57 us
  transfers between devices with their start and end apart: 1, of which 1 were waited for; matrix products, arithmetic and copies ran while one was open for 0% of the time, Pallas kernels for 4%

profile of v10, /device:TPU:6, one launch (start us, length us, event | category | flops | bytes accessed | tf_op | source)
XLA Modules:
  0.0 50.7 jit_solution(12075884504551828406)
XLA Ops:
  0.0 0.0 copy-start
  0.0 1.6 %pack.1 = (f32[16,2,8,128]{3,2,1,0:T(8,128)}, s32[3,128]{1,0:T(4,128)S(1)}, f32[3,8]{1,0:T(4,128)S(1)}, f32[3,512]{1,0:T(4,128)S(1)}) custom-call(s32[8,128]{1,0:T(8,128)} %bitcast.7, f32[8,128]{1,0:T(8,128)} %bitcast.8, f32[8,128]{1,0:T(8,128)} %bitcast.9, s32[3,128]{1,0:T(4,128)} %cell_hbm.1, f32[3,8]{1,0:T(4,128)} %station_hbm.1, f32[3,512]{1,0:T(4,128)} %w_cell_hbm.1), custom_call_target="tpu_custom_call" | custom-call | flops 2000000000 | bytes 1000000 | tf_op jit(solution)/shard_map/pack/pallas_call | solution.py:193
  1.6 0.0 copy-start.4
  1.6 0.0 copy-start.2
  1.6 13.5 %all-to-all-start = ((f32[16,2,8,128]{3,2,1,0:T(8,128)}), f32[16,2,8,128]{3,2,1,0:T(8,128)S(1)}, u32[]{:S(2)}, u32[]{:S(2)}) async-start(f32[16,2,8,128]{3,2,1,0:T(8,128)} %get-tuple-element.14), calls=%async_computation | async-start | bytes 262144 | tf_op jit(solution)/shard_map/all_to_all | solution.py:211
  15.2 0.0 copy-done.4
  15.2 0.0 copy-start.1
  15.2 0.0 copy-start.3
  15.2 0.0 copy-done
  15.2 0.0 copy-done.2
  15.2 0.6 %copy-done.1 = f32[3,512]{1,0:T(4,128)S(1)} copy-done((f32[3,512]{1,0:T(4,128)S(1)}, f32[3,512]{1,0:T(4,128)}, u32[]{:S(2)}) %copy-start.1) | copy-done | bytes 6168
  15.9 0.0 copy-done.3
  15.9 2.1 %travel.1.travel_ref = f32[8,128]{1,0:T(8,128)S(1)} custom-call(s32[3,128]{1,0:T(4,128)S(1)} %get-tuple-element.11.cell_ref, f32[3,8]{1,0:T(4,128)S(1)} %get-tuple-element.12.station_ref, f32[3,512]{1,0:T(4,128)S(1)} %get-tuple-element.13.w_cell_ref, f32[3,512]{1,0:T(4,128)S(1)} %copy-done.1, f32[1,512]{1,0:T(1,128)S(1)} %bitcast.6, ...), custom_call_target="tpu_custom_call" | custom-call | tf_op jit(solution)/shard_map/travel/pallas_call | solution.py:212
  17.9 3.9 %all-to-all-done.picks_ref = f32[16,2,8,128]{3,2,1,0:T(8,128)S(1)} async-done(((f32[16,2,8,128]{3,2,1,0:T(8,128)}), f32[16,2,8,128]{3,2,1,0:T(8,128)S(1)}, u32[]{:S(2)}, u32[]{:S(2)}) %all-to-all-start) | async-done | bytes 131104 | tf_op jit(solution)/shard_map/all_to_all | solution.py:211
  21.8 13.2 %all_to_all.15 = f32[16,3,8,128]{3,2,1,0:T(8,128)S(1)} all-to-all(f32[16,3,8,128]{3,2,1,0:T(8,128)S(1)} %join.1), channel_id=1, replica_groups={{26,28,30,0,2,4,6,8,10,12,14,16,18,20,22,24},{27,29,31,1,3,5,7,9,11,13,..., dimensions={0} | all-to-all | bytes 393216 | tf_op jit(solution)/shard_map/all_to_all | solution.py:231
  35.0 2.1 %all-gather = f32[32,3,8,128]{3,2,1,0:T(8,128)S(1)} all-gather(f32[16,3,8,128]{3,2,1,0:T(8,128)S(1)} %all_to_all.15), channel_id=2, replica_groups={{0,1},{2,3},{4,5},{6,7},{8,9},{10,11},{12,13},{14,15},{16,17},{18,19},{..., dimensions={0}, use_global_device_ids=true | all-gather | bytes 589824 | tf_op jit(solution)/shard_map/all_gather | solution.py:232
  37.1 0.6 %logit.1 = (f32[64,128]{1,0:T(8,128)S(1)}, f32[16,1,128]{2,1,0:T(1,128)S(1)}) custom-call(f32[2,16,3,8,128]{4,3,2,1,0:T(8,128)S(1)} %bitcast.5), custom_call_target="tpu_custom_call" | custom-call | tf_op jit(solution)/shard_map/logit/pallas_call | solution.py:233
  37.7 12.2 %all_to_all.16.stats_ref = f32[16,1,128]{2,1,0:T(1,128)S(1)} all-to-all(f32[16,1,128]{2,1,0:T(1,128)S(1)} %get-tuple-element.16), channel_id=1, replica_groups={{384,416,448,480,0,32,64,96,128,160,192,224,256,288,320,352},{385,417,4..., dimensions={0} | all-to-all | bytes 16384 | tf_op jit(solution)/shard_map/all_to_all | solution.py:239
  49.9 0.9 %final.1 = f32[64,128]{1,0:T(8,128)} custom-call(f32[64,128]{1,0:T(8,128)S(1)} %get-tuple-element.15.logit_ref, f32[16,1,128]{2,1,0:T(1,128)S(1)} %all_to_all.16.stats_ref), custom_call_target="tpu_custom_call" | custom-call | tf_op jit(solution)/shard_map/final/pallas_call | solution.py:240
  (2 shorter events, 0.0 us)
Async XLA Ops:
  0.0 15.2 %copy-start = (bf16[2,512,512]{2,1,0:T(8,128)(2,1)S(1)}, bf16[2,512,512]{2,1,0:T(8,128)(2,1)}, u32[]{:S(2)}) copy-start(bf16[2,512,512]{2,1,0:T(8,128)(2,1)} %w_hidden_ref.1) | copy-start | bytes 3145732
  1.6 13.6 %copy-start.4 = (bf16[512]{0:T(512)(128)(2,1)S(1)}, bf16[512]{0:T(512)(128)(2,1)}, u32[]{:S(2)}) copy-start(bf16[512]{0:T(512)(128)(2,1)} %param.18) | copy-start | bytes 3076
  1.6 13.6 %copy-start.2 = (f32[2,512]{1,0:T(2,128)S(1)}, f32[2,512]{1,0:T(2,128)}, u32[]{:S(2)}) copy-start(f32[2,512]{1,0:T(2,128)} %bias_hidden_ref.1) | copy-start | bytes 12292
  1.6 20.2 %all-to-all-start = ((f32[16,2,8,128]{3,2,1,0:T(8,128)}), f32[16,2,8,128]{3,2,1,0:T(8,128)S(1)}, u32[]{:S(2)}, u32[]{:S(2)}) async-start(f32[16,2,8,128]{3,2,1,0:T(8,128)} %get-tuple-element.14), calls=%async_computation | async-start | bytes 262144 | tf_op jit(solution)/shard_map/all_to_all | solution.py:211
  15.2 0.7 %copy-start.1 = (f32[3,512]{1,0:T(4,128)S(1)}, f32[3,512]{1,0:T(4,128)}, u32[]{:S(2)}) copy-start(f32[3,512]{1,0:T(4,128)} %w_station_ref.1) | copy-start | bytes 18436
  15.2 0.7 %copy-start.3 = (f32[512]{0:T(512)S(1)}, f32[512]{0:T(512)}, u32[]{:S(2)}) copy-start(f32[512]{0:T(512)} %param.15) | copy-start | bytes 6148
